TPU v7x, 256 devices: a whole 4x4x8 slice. The times are simulated.
256 devices in a mesh: section: 2 (over core), dp: 8 (over z), head: 16 (over y, x).
Axes of the slice: x: 4, y: 4, z: 8, core: 2. Of those that a mesh axis runs over, the one named last changes fastest.
Arguments:
- tokens: bfloat16 [2048, 1600], P('dp'), may hold values from -6 to 6
- up_weight: bfloat16 [2, 1600, 6400], P('section', 'dp', 'head'), may hold values from -0.15625 to 0.15625
- down_weight: bfloat16 [2, 6400, 1600], P('section', 'head', 'dp'), may hold values from -0.078125 to 0.078125
- neck_weight: bfloat16 [1600, 1024], replicated, may hold values from -0.15625 to 0.15625
- casc_weight: bfloat16 [3, 1024, 1024], replicated, may hold values from -0.1875 to 0.1875
- class_weight: bfloat16 [3, 1024, 80], replicated, may hold values from -0.1875 to 0.1875
- roi_bins: int32 [4096, 16], P('dp'), may hold values from 0 to 255
- positive: int32 [4096], P('dp'), may hold values 0 or 1
- targets: int32 [4096, 3], P('dp'), may hold values from 0 to 79
Outputs:
- grad_up: float32 [2, 1600, 6400], P('section', 'dp', 'head')
- grad_down: float32 [2, 6400, 1600], P('section', 'head', 'dp')
Inputs may be any that keep to these rules, and one draw needn't show every extreme that they name: `roi_bins`: the sample bins of a RoI index the 256 bins of its own image.
All inputs are finite; a program needn't handle non-finite values. No bound on the sum of `positive` on one device may be relied on, other than what follows from the above.
Results may differ from a plain program's by a relative error of at most 0.004.
Values may be sent and summed in bfloat16 or wider, within the bound.
A program may use at most 128 MiB of HBM per device.

v0:
```python
import jax
import jax.numpy as jnp
from jax import lax
from jax.sharding import PartitionSpec as P

MICRO = 4


epsilon = 1e-06


def passed_along(array, axis, by):
    length = lax.axis_size(axis)
    pairs = [(i, i + by) for i in range(length) if 0 <= i + by < length]
    return lax.ppermute(array, axis, pairs)


def smooth_act(values):
    return jax.nn.gelu(values, approximate=True)


def smooth_slope(values):
    return jax.jvp(smooth_act, (values,), (jnp.ones_like(values),))[1]


def normalize(values):
    centre = values - jnp.mean(values, axis=-1, keepdims=True)
    inv_std = lax.rsqrt(jnp.mean(centre * centre, axis=-1, keepdims=True) + epsilon)
    return (centre * inv_std, inv_std)


def norm_back(grad_in, scaled, inv_std):
    mean_one = jnp.mean(grad_in, axis=-1, keepdims=True)
    mean_two = jnp.mean(grad_in * scaled, axis=-1, keepdims=True)
    return inv_std * (grad_in - mean_one - scaled * mean_two)


def transpose_dot(left_side, right_side):
    return lax.dot_general(
        left_side, right_side, (((0,), (0,)), ((), ())), preferred_element_type=jnp.float32
    )


def dot_trans(left_side, right_side):
    return lax.dot_general(
        left_side, right_side, (((1,), (1,)), ((), ())), preferred_element_type=jnp.float32
    )


def pool_matrix(sample_bins, bins_total):
    matches = sample_bins[:, :, None] == jnp.arange(bins_total, dtype=jnp.int32)[None, None, :]
    counted = jnp.sum(matches.astype(jnp.float32), axis=1)
    return (counted / sample_bins.shape[1]).astype(jnp.bfloat16)


def target_table(labels, positive, classes_total):
    matches = labels[:, :, None] == jnp.arange(classes_total, dtype=jnp.int32)[None, None, :]
    return matches.astype(jnp.float32) * positive[:, None, None].astype(jnp.float32)


def head_pass(pooled, casc_weight, class_weight, wanted):
    current = pooled
    inner_list = []
    outer_list = []
    for level_num in range(casc_weight.shape[0]):
        mixed_rows = jnp.dot(current, casc_weight[level_num], preferred_element_type=jnp.float32)
        inner_list.append(mixed_rows)
        current = (current.astype(jnp.float32) + smooth_act(mixed_rows)).astype(jnp.bfloat16)
        logits = jnp.dot(current, class_weight[level_num], preferred_element_type=jnp.float32)
        outer_list.append((jax.nn.sigmoid(logits) - wanted[:, level_num]).astype(jnp.bfloat16))
    running = jnp.zeros(pooled.shape, jnp.float32)
    for level_num in reversed(range(casc_weight.shape[0])):
        running = running + dot_trans(outer_list[level_num], class_weight[level_num])
        through = (running * smooth_slope(inner_list[level_num])).astype(jnp.bfloat16)
        running = running + dot_trans(through, casc_weight[level_num])
    return running.astype(jnp.bfloat16)


def head_total(values):
    return lax.psum(values, "head")


def pass_on(values, offset):
    return passed_along(values, "section", offset)


def keep_slot(stack_arr, value_arr, slot_pos, running):
    old_value = lax.dynamic_index_in_dim(stack_arr, slot_pos, 0, keepdims=False)
    new_value = jnp.where(running, value_arr, old_value)
    return lax.dynamic_update_index_in_dim(stack_arr, new_value, slot_pos, 0)


def take_slot(stack_arr, slot_pos):
    return lax.dynamic_index_in_dim(stack_arr, slot_pos, 0, keepdims=False)


def per_device(
    tokens,
    up_weight,
    down_weight,
    neck_weight,
    casc_weight,
    class_weight,
    roi_bins,
    positive,
    targets,
):
    segment_pos = lax.axis_index("section")
    segment_count = lax.axis_size("section")
    last_segment = segment_count - 1
    head_pos = lax.axis_index("head")
    head_count = lax.axis_size("head")
    up_full, down_full = (
        lax.all_gather(up_weight, "dp", axis=1, tiled=True),
        lax.all_gather(down_weight, "dp", axis=2, tiled=True),
    )
    up_local = up_full[0]
    down_local = down_full[0]
    bins_total = tokens.shape[0]
    tok_rows = bins_total // MICRO
    width = tokens.shape[1]
    hidden_local = up_local.shape[1]
    micro_batches = tokens.reshape(MICRO, tok_rows, width)
    inputs_kept = jnp.zeros((MICRO, tok_rows, width), jnp.bfloat16)
    normed_kept = jnp.zeros((MICRO, tok_rows, width), jnp.bfloat16)
    before_kept = jnp.zeros((MICRO, tok_rows, hidden_local), jnp.float32)
    outputs_kept = jnp.zeros((MICRO, tok_rows, width), jnp.bfloat16)
    incoming = jnp.zeros((tok_rows, width), jnp.bfloat16)
    tick_count = MICRO + segment_count - 1
    for tick_num in range(tick_count):
        micro_pos = tick_num - segment_pos
        running = (micro_pos >= 0) & (micro_pos < MICRO)
        slot_pos = jnp.clip(micro_pos, 0, MICRO - 1)
        current = jnp.where(segment_pos == 0, micro_batches[min(tick_num, MICRO - 1)], incoming)
        scaled, inv_std = normalize(current.astype(jnp.float32))
        normed = scaled.astype(jnp.bfloat16)
        before = jnp.dot(normed, up_local, preferred_element_type=jnp.float32)
        active = smooth_act(before).astype(jnp.bfloat16)
        partial_value = jnp.dot(active, down_local, preferred_element_type=jnp.float32)
        output = (current.astype(jnp.float32) + head_total(partial_value)).astype(jnp.bfloat16)
        inputs_kept = keep_slot(inputs_kept, current, slot_pos, running)
        normed_kept = keep_slot(normed_kept, normed, slot_pos, running)
        before_kept = keep_slot(before_kept, before, slot_pos, running)
        outputs_kept = keep_slot(outputs_kept, output, slot_pos, running)
        incoming = pass_on(output, 1)
    features = jnp.dot(
        outputs_kept.reshape(bins_total, width), neck_weight, preferred_element_type=jnp.float32
    ).astype(jnp.bfloat16)
    row_share = roi_bins.shape[0] // head_count
    mine_bins = lax.dynamic_slice_in_dim(roi_bins, head_pos * row_share, row_share, 0)
    pooling = pool_matrix(mine_bins, bins_total)
    pooled = jnp.dot(pooling, features, preferred_element_type=jnp.float32).astype(jnp.bfloat16)
    wanted_all = target_table(targets, positive, class_weight.shape[2])
    wanted = lax.dynamic_slice_in_dim(wanted_all, head_pos * row_share, row_share, 0)
    pooled_grad = head_pass(pooled, casc_weight, class_weight, wanted)
    feature_grad = lax.psum(transpose_dot(pooling, pooled_grad), "head").astype(jnp.bfloat16)
    upstream_all = (
        dot_trans(feature_grad, neck_weight).astype(jnp.bfloat16).reshape(MICRO, tok_rows, width)
    )
    upstream_kept = jnp.zeros((MICRO, tok_rows, width), jnp.bfloat16)
    hidden_kept = jnp.zeros((MICRO, tok_rows, hidden_local), jnp.bfloat16)
    incoming = jnp.zeros((tok_rows, width), jnp.bfloat16)
    for tick_num in range(tick_count):
        micro_pos = tick_num - (last_segment - segment_pos)
        running = (micro_pos >= 0) & (micro_pos < MICRO)
        slot_pos = jnp.clip(micro_pos, 0, MICRO - 1)
        upstream = jnp.where(
            segment_pos == last_segment, take_slot(upstream_all, slot_pos), incoming
        )
        current = take_slot(inputs_kept, slot_pos)
        before = take_slot(before_kept, slot_pos)
        scaled, inv_std = normalize(current.astype(jnp.float32))
        hidden_grad = (dot_trans(upstream, down_local) * smooth_slope(before)).astype(jnp.bfloat16)
        grad_term = dot_trans(hidden_grad, up_local)
        normed_grad = head_total(grad_term)
        upstream_out = (
            upstream.astype(jnp.float32) + norm_back(normed_grad, scaled, inv_std)
        ).astype(jnp.bfloat16)
        upstream_kept = keep_slot(upstream_kept, upstream, slot_pos, running)
        hidden_kept = keep_slot(hidden_kept, hidden_grad, slot_pos, running)
        incoming = pass_on(upstream_out, -1)
    flat_normed = normed_kept.reshape(bins_total, width)
    flat_hidden = hidden_kept.reshape(bins_total, hidden_local)
    flat_active = smooth_act(before_kept).astype(jnp.bfloat16).reshape(bins_total, hidden_local)
    flat_upstream = upstream_kept.reshape(bins_total, width)
    local_up = transpose_dot(flat_normed, flat_hidden)[None]
    local_down = transpose_dot(flat_active, flat_upstream)[None]
    summed_up, summed_down = (
        lax.psum_scatter(local_up, "dp", scatter_dimension=1, tiled=True),
        lax.psum_scatter(local_down, "dp", scatter_dimension=2, tiled=True),
    )
    return (summed_up, summed_down)


def solution(mesh):
    return jax.shard_map(
        per_device,
        mesh=mesh,
        in_specs=(
            P("dp", None),
            P("section", "dp", "head"),
            P("section", "head", "dp"),
            P(),
            P(),
            P(),
            P("dp", None),
            P("dp"),
            P("dp", None),
        ),
        out_specs=(P("section", "dp", "head"), P("section", "head", "dp")),
        check_vma=False,
    )
```

profile of v0, /device:TPU:32, one launch (start us, length us, event | category | flops | bytes accessed | tf_op | source)
XLA Modules:
  0.0 1258.7 jit_solution(2703746511931020916)
XLA Ops:
  10.1 2.9 fusion.506
  24.8 33.8 %all-gather.5.cloned.1.call-done = bf16[1,400,1600]{1,0,2:T(2,128)(2,1)} async-done(((bf16[1,400,200]{1,0,2:T(2,128)(2,1)}), bf16[1,400,1600]{1,0,2:T(2,128)(2,1)}) %all-gather.5.cloned.1.call-update) | async-done | bytes 1280016 | tf_op jit(solution)/shard_map/all_gather | solution.py:115
  58.6 8.3 copy.49
  66.9 32.5 %all-gather.3.cloned.1.call-done = bf16[1,1600,400]{2,1,0:T(8,128)(2,1)} async-done(((bf16[1,200,400]{2,1,0:T(8,128)(2,1)}), bf16[1,1600,400]{2,1,0:T(8,128)(2,1)}) %all-gather.3.cloned.1.call-update) | async-done | bytes 1280016 | tf_op jit(solution)/shard_map/all_gather | solution.py:114
  100.3 2.5 bitcast_dynamic-update-slice_fusion.22
  105.8 91.9 %all-reduce.11.cloned.1.call-done = f32[64,1600]{1,0:T(8,128)} async-done(((f32[64,1600]{1,0:T(8,128)}), f32[64,1600]{1,0:T(8,128)}) %all-reduce.11.cloned.1.call-update) | async-done | bytes 409616 | tf_op jit(solution)/shard_map/psum | solution.py:80
  213.0 89.5 %all-reduce.13.cloned.1.call-done = f32[64,1600]{1,0:T(8,128)} async-done(((f32[64,1600]{1,0:T(8,128)}), f32[64,1600]{1,0:T(8,128)}) %all-reduce.13.cloned.1.call-update) | async-done | bytes 409616 | tf_op jit(solution)/shard_map/psum | solution.py:80
  302.5 2.3 bitcast_dynamic-update-slice_fusion.11
  315.6 88.5 %all-reduce.15.cloned.1.call-done = f32[64,1600]{1,0:T(8,128)} async-done(((f32[64,1600]{1,0:T(8,128)}), f32[64,1600]{1,0:T(8,128)}) %all-reduce.15.cloned.1.call-update) | async-done | bytes 409616 | tf_op jit(solution)/shard_map/psum | solution.py:80
  417.7 88.6 %all-reduce.17.cloned.1.call-done = f32[64,1600]{1,0:T(8,128)} async-done(((f32[64,1600]{1,0:T(8,128)}), f32[64,1600]{1,0:T(8,128)}) %all-reduce.17.cloned.1.call-update) | async-done | bytes 409616 | tf_op jit(solution)/shard_map/psum | solution.py:80
  506.3 2.3 bitcast_dynamic-update-slice_fusion.9
  520.7 89.4 %all-reduce.19.cloned.1.call-done = f32[64,1600]{1,0:T(8,128)} async-done(((f32[64,1600]{1,0:T(8,128)}), f32[64,1600]{1,0:T(8,128)}) %all-reduce.19.cloned.1.call-update) | async-done | bytes 409616 | tf_op jit(solution)/shard_map/psum | solution.py:80
  612.2 2.4 fusion.99
  614.6 2.7 add_convert_fusion.2
  617.4 2.7 add_convert_fusion.1
  624.2 3.0 fusion.78
  629.2 3.1 fusion.75
  633.8 3.6 fusion.101
  637.4 86.0 %all-reduce.28 = bf16[256,1024]{1,0:T(8,128)(2,1)} all-reduce(f32[256,1024]{1,0:T(8,128)} %fusion.101), channel_id=1, replica_groups=mesh['section'=2,'dp'=8,'head'=16] {'head'}, use_global_device_ids=true, to_apply=%region_16.17 | all-reduce | flops 262144 | bytes 1572864 | tf_op jit(solution)/shard_map/psum | solution.py:156
  723.4 3.0 convolution_convert_fusion
  736.2 87.9 %all-reduce.21.cloned.1.call-done = f32[64,1600]{1,0:T(8,128)} async-done(((f32[64,1600]{1,0:T(8,128)}), f32[64,1600]{1,0:T(8,128)}) %all-reduce.21.cloned.1.call-update) | async-done | bytes 409616 | tf_op jit(solution)/shard_map/psum | solution.py:80
  824.0 2.6 fusion.200
  838.2 92.1 %all-reduce.23.cloned.1.call-done = f32[64,1600]{1,0:T(8,128)} async-done(((f32[64,1600]{1,0:T(8,128)}), f32[64,1600]{1,0:T(8,128)}) %all-reduce.23.cloned.1.call-update) | async-done | bytes 409616 | tf_op jit(solution)/shard_map/psum | solution.py:80
  943.0 92.1 %all-reduce.25.cloned.1.call-done = f32[64,1600]{1,0:T(8,128)} async-done(((f32[64,1600]{1,0:T(8,128)}), f32[64,1600]{1,0:T(8,128)}) %all-reduce.25.cloned.1.call-update) | async-done | bytes 409616 | tf_op jit(solution)/shard_map/psum | solution.py:80
  1046.6 93.4 %all-reduce.27.cloned.1.call-done = f32[64,1600]{1,0:T(8,128)} async-done(((f32[64,1600]{1,0:T(8,128)}), f32[64,1600]{1,0:T(8,128)}) %all-reduce.27.cloned.1.call-update) | async-done | bytes 409616 | tf_op jit(solution)/shard_map/psum | solution.py:80
  1146.9 2.5 fusion.109
  1149.4 3.5 convolution_bitcast_fusion
  1155.6 3.5 convolution_bitcast_fusion.1
  1159.1 8.6 copy.57
  1167.8 4.0 copy.67
  1171.8 26.7 %reduce-scatter.7.cloned.1.call-done = f32[200,400]{1,0:T(8,128)} async-done(((f32[1600,400]{1,0:T(8,128)}), f32[200,400]{1,0:T(8,128)}) %reduce-scatter.7.cloned.1.call-update) | async-done | bytes 320016
  1200.6 47.7 %reduce-scatter.9.cloned.1.call-done = f32[200,400]{1,0:T(8,128)} async-done(((f32[1600,400]{1,0:T(8,128)}), f32[200,400]{1,0:T(8,128)}) %reduce-scatter.9.cloned.1.call-update) | async-done | bytes 320016
  (252 shorter events, 140.6 us)
Async XLA Ops:
  7.2 605.1 %copy-start = (bf16[1600,1024]{1,0:T(8,128)(2,1)S(1)}, bf16[1600,1024]{1,0:T(8,128)(2,1)}, u32[]{:S(2)}) copy-start(bf16[1600,1024]{1,0:T(8,128)(2,1)} %param.12) | copy-start | bytes 9830404
  7.2 51.4 %all-gather.5.cloned.1.call-start = ((), (), s32[]{:S(2)}) async-start(), calls=%async_computation.3 | async-start | bytes 3686400 | tf_op jit(solution)/shard_map/all_gather | solution.py:115
  9.3 90.2 %all-gather.3.cloned.1.call-start = ((), (), s32[]{:S(2)}) async-start(), calls=%async_computation.2 | async-start | bytes 1843200 | tf_op jit(solution)/shard_map/all_gather | solution.py:114
  10.1 187.6 %all-reduce.11.cloned.1.call-start = ((), (), s32[]{:S(2)}) async-start(), calls=%async_computation.4 | async-start | bytes 851968 | tf_op jit(solution)/shard_map/psum | solution.py:80
  104.0 198.4 %all-reduce.13.cloned.1.call-start = ((), (), s32[]{:S(2)}) async-start(), calls=%async_computation.5 | async-start | bytes 851968 | tf_op jit(solution)/shard_map/psum | solution.py:80
  200.4 3.9 collective-permute-start
  208.9 195.2 %all-reduce.15.cloned.1.call-start = ((), (), s32[]{:S(2)}) async-start(), calls=%async_computation.6 | async-start | bytes 851968 | tf_op jit(solution)/shard_map/psum | solution.py:80
  304.7 2.4 collective-permute-start.1
  310.5 195.8 %all-reduce.17.cloned.1.call-start = ((), (), s32[]{:S(2)}) async-start(), calls=%async_computation.7 | async-start | bytes 851968 | tf_op jit(solution)/shard_map/psum | solution.py:80
  406.4 2.9 collective-permute-start.2
  412.8 197.3 %all-reduce.19.cloned.1.call-start = ((), (), s32[]{:S(2)}) async-start(), calls=%async_computation.8 | async-start | bytes 851968 | tf_op jit(solution)/shard_map/psum | solution.py:80
  506.3 8.0 copy-start.4
  506.3 8.0 copy-start.25
  508.6 4.6 collective-permute-start.3
  516.6 307.4 %all-reduce.21.cloned.1.call-start = ((), (), s32[]{:S(2)}) async-start(), calls=%async_computation.9 | async-start | bytes 851968 | tf_op jit(solution)/shard_map/psum | solution.py:80
  518.9 305.1 %copy-start.32 = (f32[64]{0:T(128)}, f32[64]{0:T(128)S(1)}, u32[]{:S(2)}) copy-start(f32[64]{0:T(128)S(1)} %broadcast_multiply_fusion.2) | copy-start | bytes 772
  520.7 303.4 %copy-start.34 = (f32[64]{0:T(128)}, f32[64]{0:T(128)S(1)}, u32[]{:S(2)}) copy-start(f32[64]{0:T(128)S(1)} %broadcast_multiply_fusion.5) | copy-start | bytes 772
  730.6 99.8 %copy-start.21 = (bf16[4,64,400]{2,1,0:T(8,128)(2,1)}, bf16[4,64,400]{2,1,0:T(8,128)(2,1)S(1)}, u32[]{:S(2)}) copy-start(bf16[4,64,400]{2,1,0:T(8,128)(2,1)S(1)} %get-tuple-element.72) | copy-start | bytes 614404
  732.1 198.2 %all-reduce.23.cloned.1.call-start = ((), (), s32[]{:S(2)}) async-start(), calls=%async_computation.10 | async-start | bytes 851968 | tf_op jit(solution)/shard_map/psum | solution.py:80
  732.8 95.2 %copy-start.35 = (f32[64]{0:T(128)}, f32[64]{0:T(128)S(1)}, u32[]{:S(2)}) copy-start(f32[64]{0:T(128)S(1)} %broadcast_multiply_fusion.8) | copy-start | bytes 772
  824.0 9.2 copy-start.14
  824.0 9.2 copy-start.28
  828.0 3.5 collective-permute-start.4
  836.7 198.4 %all-reduce.25.cloned.1.call-start = ((), (), s32[]{:S(2)}) async-start(), calls=%async_computation.11 | async-start | bytes 851968 | tf_op jit(solution)/shard_map/psum | solution.py:80
  930.2 7.9 copy-start.15
  933.0 3.4 collective-permute-start.5
  941.6 198.4 %all-reduce.27.cloned.1.call-start = ((), (), s32[]{:S(2)}) async-start(), calls=%async_computation.12 | async-start | bytes 851968 | tf_op jit(solution)/shard_map/psum | solution.py:80
  1037.9 3.4 collective-permute-start.6
  1045.1 94.9 %copy-start.33 = (f32[64]{0:T(128)S(1)}, f32[64]{0:T(128)}, u32[]{:S(2)}) copy-start(f32[64]{0:T(128)} %copy-done.32) | copy-start | bytes 772
  1046.5 152.0 %reduce-scatter.7.cloned.1.call-start = ((), (), s32[]{:S(2)}) async-start(), calls=%async_computation.13 | async-start | bytes 3686400
  1143.3 3.6 collective-permute-start.7
  1152.9 95.3 %reduce-scatter.9.cloned.1.call-start = ((), (), s32[]{:S(2)}) async-start(), calls=%async_computation.14 | async-start | bytes 3686400
  (31 other events, 124.7 us)
Sparse Core Ops, SparseCore 0:
  10.4 48.1 all-gather.4
  60.4 39.0 all-gather.2
  104.2 93.4 all-reduce.10
  209.1 93.3 all-reduce.12
  310.7 93.4 all-reduce.14
  412.9 93.3 all-reduce.16
  516.7 93.3 all-reduce.18
  732.2 91.8 all-reduce.20
  836.9 93.3 all-reduce.22
  941.7 93.3 all-reduce.24
  1046.6 93.3 all-reduce.26
  1153.1 45.3 reduce-scatter.6
  1201.2 46.9 reduce-scatter.8
where the time goes:
time: 1260 us
  waiting for transfers between devices  959 us (76%)
  blocking collectives  86 us (7%)
  local copies, waits for them, and re-layouts  77.3 us (6%)
  matrix products  64.1 us (5%)
  other arithmetic  45.5 us (4%)
  between operations  14.5 us (1%)
    psum x9, waiting for transfers between devices, head_total(): return lax.psum(values, 'head')  813 us
    psum x1, blocking collectives, per_device(): lax.psum(transpose_dot(pooling, pooled_grad), 'head').astype(jnp.bfloat16)  86 us
    unnamed x15, waiting for transfers between devices  75.2 us
    all_gather x1, waiting for transfers between devices, per_device(): lax.all_gather(down_weight, 'dp', axis=2, tiled=True)  33.8 us
    all_gather x1, waiting for transfers between devices, per_device(): lax.all_gather(up_weight, 'dp', axis=1, tiled=True)  32.5 us
    dot_general x15, matrix products, dot_trans(): lax.dot_general(left_side, right_side, (((1,), (1,)), ((), ())), preferre...  31 us
    dynamic_slice x23, local copies, waits for them, and re-layouts, keep_slot(): old_value = lax.dynamic_index_in_dim(stack_arr, slot_pos, 0, keepdims=False)  29.6 us
    unnamed x95, local copies, waits for them, and re-layouts  29.5 us
  transfers between devices with their start and end apart: 21, of which 18 were waited for; matrix products, arithmetic and copies ran while one was open for 6% of the time, Pallas kernels for 0%

commit v1 on v0

v1 whole, which is shorter than its diff:
```python
import jax
import jax.numpy as jnp
from jax import lax
from jax.experimental import pallas as pl
from jax.experimental.pallas import tpu as pltpu
from jax.sharding import PartitionSpec as P

MESH = pl.DeviceIdType.MESH
EPS = 1e-06
BF = jnp.bfloat16
F32 = jnp.float32


def dot(a, b):
    return jnp.dot(a, b, preferred_element_type=F32)


def dot_rt(a, b):
    return lax.dot_general(a, b, (((1,), (1,)), ((), ())), preferred_element_type=F32)


def dot_lt(a, b):
    return lax.dot_general(a, b, (((0,), (0,)), ((), ())), preferred_element_type=F32)


def gelu_both(z):
    c = 0.7978845608028654
    zz = z * z
    t = jnp.tanh(c * z * (1.0 + 0.044715 * zz))
    half = 0.5 * (1.0 + t)
    slope = half + (0.5 * c) * z * (1.0 - t * t) * (1.0 + (3 * 0.044715) * zz)
    return z * half, slope


def norm_rows(x):
    centre = x - jnp.mean(x, axis=-1, keepdims=True)
    inv = lax.rsqrt(jnp.mean(centre * centre, axis=-1, keepdims=True) + EPS)
    return centre * inv, inv


def make_kernel(nd, nh, dims):
    rows, width, wsl, hid, chan, cls, levels, rois, ksamp = dims
    rb = rows // nh
    qb = rois // nh
    n_right = nd // 2
    n_left = nd - 1 - n_right

    def kernel(
        tokens, up, down, neck, casc, clsw, bins, labels, gup, gdn,
        upg, dng, xb, nrm, slope, act, hg, part, rs_a, rs_d, yall, ppart, prec, pg,
        xrow, nsb, nzr, nsl, ysb, ysb1, yzr, ysl, neckv, cascv, clsr, clsv, terms, binv, labv, poolv,
        lsem, ss, rs, zgo,
    ):
        s = lax.axis_index("section")
        d = lax.axis_index("dp")
        h = lax.axis_index("head")
        myrows = pl.ds(pl.multiple_of(h * rb, rb), rb)
        myrois = pl.ds(pl.multiple_of(h * qb, qb), qb)

        def loop(a, b, body):
            def step(k, c):
                body(k)
                return c

            lax.fori_loop(a, b, step, 0)

        def plane(row, src, dst, core):
            def make(k):
                t = lax.rem(h + k, nh)
                return pltpu.make_async_remote_copy(
                    src_ref=src(t), dst_ref=dst(k), send_sem=ss.at[row, k], recv_sem=rs.at[row, k],
                    device_id=(core, d, t), device_id_type=MESH,
                )

            return make

        def column(row, src, dst, core):
            def make(k):
                t = lax.rem(d + k, nd)
                return pltpu.make_async_remote_copy(
                    src_ref=src(t), dst_ref=dst(k), send_sem=ss.at[row, k], recv_sem=rs.at[row, k],
                    device_id=(core, t, h), device_id_type=MESH,
                )

            return make

        def ring(row, buf, relative, rights, lefts):
            def slot(j):
                return j if relative else lax.rem(d - j + nd, nd)

            def right(t):
                return pltpu.make_async_remote_copy(
                    src_ref=buf.at[slot(t)], dst_ref=buf.at[t + 1 if relative else slot(t)],
                    send_sem=ss.at[row, t + 1], recv_sem=rs.at[row, t + 1],
                    device_id=(s, lax.rem(d + 1, nd), h), device_id_type=MESH,
                )

            def left(t):
                j = (nd - t) % nd
                return pltpu.make_async_remote_copy(
                    src_ref=buf.at[slot(j)], dst_ref=buf.at[nd - 1 - t if relative else slot(j)],
                    send_sem=ss.at[row, nd - 1 - t], recv_sem=rs.at[row, nd - 1 - t],
                    device_id=(s, lax.rem(d + nd - 1, nd), h), device_id_type=MESH,
                )

            return [(right, rights), (left, lefts)]

        def ring_step(chains, t):
            for make, count in chains:
                if t < count:
                    if t > 0:
                        make(t - 1).wait_recv()
                    make(t).start()

        def ring_last(chains):
            for make, count in chains:
                make(count - 1).wait_recv()

        def ring_sent(chains):
            for make, count in chains:
                for t in range(count):
                    make(t).wait_send()

        load_up = pltpu.make_async_copy(up.at[0], upg.at[d], lsem.at[0])
        load_down = pltpu.make_async_copy(down.at[0], dng.at[d], lsem.at[1])
        load_up.start()
        load_down.start()
        barrier = pltpu.get_barrier_semaphore()

        def greet_plane(k):
            pl.semaphore_signal(barrier, inc=1, device_id=(s, d, lax.rem(h + k, nh)), device_id_type=MESH)

        def greet_plane_other(k):
            pl.semaphore_signal(barrier, inc=1, device_id=(1 - s, d, lax.rem(h + k, nh)), device_id_type=MESH)

        def greet_column(k):
            pl.semaphore_signal(barrier, inc=1, device_id=(s, lax.rem(d + k, nd), h), device_id_type=MESH)
            pl.semaphore_signal(barrier, inc=1, device_id=(1 - s, lax.rem(d + k, nd), h), device_id_type=MESH)

        loop(1, nd, greet_column)
        loop(1, nh, greet_plane)
        loop(0, nh, greet_plane_other)

        load_tok = pltpu.make_async_copy(tokens, xb, lsem.at[2])
        load_neck = pltpu.make_async_copy(neck, neckv, lsem.at[3])
        load_casc = pltpu.make_async_copy(casc, cascv, lsem.at[4])
        load_cls = pltpu.make_async_copy(clsw, clsr, lsem.at[5])
        load_bins = pltpu.make_async_copy(bins, binv, lsem.at[6])
        load_lab = pltpu.make_async_copy(labels, labv, lsem.at[7])
        load_tok.start()

        @pl.when(s == 1)
        def _():
            for c in (load_bins, load_lab, load_neck, load_casc, load_cls):
                c.start()

        load_up.wait()
        load_down.wait()
        pl.semaphore_wait(barrier, 2 * (nd - 1) + 2 * nh - 1)

        chains = ring(0, upg, False, n_right, n_left) + ring(1, dng, False, n_left, n_right)

        send_a = plane(2, lambda t: part.at[pl.ds(pl.multiple_of(t * rb, rb), rb)], lambda k: rs_a.at[k], 1)
        send_n = plane(3, lambda t: nrm.at[myrows], lambda k: nrm.at[myrows], 1)
        send_p = plane(4, lambda t: ppart.at[pl.ds(pl.multiple_of(t * qb, qb), qb)], lambda k: prec.at[k], 1)
        send_g = plane(5, lambda t: pg.at[myrois], lambda k: pg.at[myrois], 1)
        send_d = plane(6, lambda t: part.at[pl.ds(pl.multiple_of(t * rb, rb), rb)], lambda k: rs_d.at[k], 1)
        send_y = plane(7, lambda t: yall.at[myrows], lambda k: yall.at[myrows], 0)
        spread_n = plane(8, lambda t: nsl.at[:, myrows, :], lambda k: nsl.at[:, myrows, :], s)
        spread_y = plane(9, lambda t: ysl.at[:, myrows, :], lambda k: ysl.at[:, myrows, :], s)
        cross_n = column(10, lambda t: nsb.at[t], lambda k: nzr.at[k], s)
        cross_y2 = column(11, lambda t: ysb.at[t], lambda k: yzr.at[k], 1)
        cross_y1 = column(14, lambda t: ysb1.at[t], lambda k: yzr.at[k], 0)
        cross_act = column(12, lambda t: act.at[0], lambda k: act.at[k], s)
        cross_hg = column(13, lambda t: hg.at[0], lambda k: hg.at[k], 1)
        hg_ring = ring(13, hg, True, n_right, n_left)

        def start(make, a, b):
            loop(a, b, lambda k: make(k).start())

        def arrived(make, a, b):
            loop(a, b, lambda k: make(k).wait_recv())

        def sent(make, a, b):
            loop(a, b, lambda k: make(k).wait_send())

        def lanes(j):
            return slice(j * wsl, (j + 1) * wsl)

        def forward():
            before = dot(nrm[:, lanes(0)], upg[0])
            for j in range(1, nd):
                before = before + dot(nrm[:, lanes(j)], upg[j])
            value, rise = gelu_both(before)
            slope[...] = rise
            act[0] = value.astype(BF)

        def down_sum():
            active = act[0]
            for j in range(nd):
                part[:, lanes(j)] = dot(active, dng[j]).astype(BF)

        def backward():
            grad = dot_rt(yall[:, lanes(0)], dng[0])
            for j in range(1, nd):
                grad = grad + dot_rt(yall[:, lanes(j)], dng[j])
            hg[0] = (grad * slope[...]).astype(BF)

        def slots(dst, values):
            for j in range(nd):
                dst[j] = values[:, lanes(j)]

        def up_grad():
            total = dot_lt(nsl[0], hg[0])
            for j in range(1, nd):
                total = total + dot_lt(nsl[j], hg[j])
            gup[0] = total

        def down_grad():
            total = dot_lt(act[0], ysl[0])
            for j in range(1, nd):
                total = total + dot_lt(act[j], ysl[j])
            gdn[0] = total

        @pl.when(s == 0)
        def _():
            ring_step(chains, 0)
            load_tok.wait()
            nrm[...] = norm_rows(xb[...].astype(F32))[0].astype(BF)
            slots(nsb, nrm[myrows, :])
            for t in range(1, n_right):
                ring_step(chains, t)
            ring_last(chains)
            forward()
            down_sum()
            start(send_a, 0, nh)
            ring_sent(chains)
            pl.semaphore_signal(zgo, inc=1, device_id=(1, d, h), device_id_type=MESH)
            start(cross_n, 1, nd)
            pl.semaphore_wait(zgo, 1)
            start(cross_act, 1, nd)
            nsl[0, myrows, :] = nsb[d]
            arrived(cross_n, 1, nd)
            for j in range(1, nd):
                nsl[j, myrows, :] = nzr[j]
            sent(send_a, 0, nh)
            start(spread_n, 1, nh)
            arrived(cross_act, 1, nd)
            arrived(spread_n, 1, nh)
            sent(cross_n, 1, nd)
            sent(cross_act, 1, nd)
            sent(spread_n, 1, nh)
            arrived(send_y, 0, nh)
            backward()
            ring_step(hg_ring, 0)
            arrived(cross_y1, 0, nd)
            for j in range(nd):
                ysl[j, myrows, :] = yzr[j]
            start(spread_y, 1, nh)
            for t in range(1, n_right):
                ring_step(hg_ring, t)
            arrived(spread_y, 1, nh)
            down_grad()
            ring_last(hg_ring)
            up_grad()
            ring_sent(hg_ring)
            sent(spread_y, 1, nh)

        @pl.when(s == 1)
        def _():
            load_bins.wait()
            spots = lax.broadcasted_iota(jnp.int32, (rois, rows), 1)
            found = binv[...]
            count = jnp.zeros((rois, rows), F32)
            for j in range(ksamp):
                count = count + jnp.where(found[:, j : j + 1] == spots, 1.0, 0.0)
            poolv[...] = (count * (1.0 / ksamp)).astype(BF)
            load_tok.wait()
            load_lab.wait()
            load_neck.wait()
            load_casc.wait()
            load_cls.wait()
            clsv[...] = jnp.zeros(clsv.shape, BF)
            clsv[:, :, 0:cls] = clsr[...]
            pl.semaphore_wait(zgo, 1)
            for t in range(n_right):
                ring_step(chains, t)
            ring_last(chains)
            ring_sent(chains)
            pl.semaphore_signal(zgo, inc=1, device_id=(0, d, h), device_id_type=MESH)

            total = xb[myrows, :].astype(F32)
            arrived(send_a, 0, nh)
            for k in range(nh):
                total = total + rs_a[k].astype(F32)
            xrow[...] = total.astype(BF)
            normed = norm_rows(xrow[...].astype(F32))[0].astype(BF)
            nrm[myrows, :] = normed
            start(send_n, 1, nh)
            slots(nsb, normed)
            start(cross_n, 1, nd)
            arrived(send_n, 1, nh)
            forward()
            start(cross_act, 1, nd)
            down_sum()
            part[myrows, :] = (part[myrows, :].astype(F32) + xrow[...].astype(F32)).astype(BF)
            features = dot(part[...], neckv[...]).astype(BF)
            ppart[...] = dot(poolv[...], features).astype(BF)
            start(send_p, 1, nh)
            nsl[0, myrows, :] = nsb[d]
            arrived(cross_n, 1, nd)
            for j in range(1, nd):
                nsl[j, myrows, :] = nzr[j]
            total = ppart[myrois, :].astype(F32)
            arrived(send_p, 1, nh)
            start(spread_n, 1, nh)
            for k in range(1, nh):
                total = total + prec[k].astype(F32)

            current = total.astype(BF)
            wanted = labv[myrois, :]
            classes = lax.broadcasted_iota(jnp.int32, (qb, 128), 1)
            rises = []
            errors = []
            for j in range(levels):
                value, rise = gelu_both(dot(current, cascv[j]))
                rises.append(rise)
                current = (current.astype(F32) + value).astype(BF)
                logits = dot(current, clsv[j])
                hit = jnp.where(wanted[:, j : j + 1] == classes, 1.0, 0.0)
                errors.append(jnp.where(classes < cls, jax.nn.sigmoid(logits) - hit, 0.0).astype(BF))
                terms[2 * j] = dot_rt(errors[j], clsv[j])
            running = jnp.zeros((qb, chan), F32)
            for j in reversed(range(levels)):
                running = running + terms[2 * j]
                through = (running * rises[j]).astype(BF)
                terms[2 * j + 1] = dot_rt(through, cascv[j])
                running = running + terms[2 * j + 1]
            pg[myrois, :] = running.astype(BF)
            start(send_g, 1, nh)
            arrived(send_g, 1, nh)
            feature_grad = dot_lt(poolv[...], pg[...]).astype(BF)
            yall[...] = dot_rt(feature_grad, neckv[...]).astype(BF)

            backward()
            start(cross_hg, 1, nd)
            hidden = hg[0]
            for j in range(nd):
                part[:, lanes(j)] = dot_rt(hidden, upg[j]).astype(BF)
            start(send_d, 1, nh)
            slots(ysb, yall[myrows, :])
            start(cross_y2, 1, nd)
            scaled, inv = norm_rows(xrow[...].astype(F32))
            total = part[myrows, :].astype(F32)
            arrived(send_d, 1, nh)
            for k in range(1, nh):
                total = total + rs_d[k].astype(F32)
            mean_one = jnp.mean(total, axis=-1, keepdims=True)
            mean_two = jnp.mean(total * scaled, axis=-1, keepdims=True)
            y_one = (yall[myrows, :].astype(F32) + inv * (total - mean_one - scaled * mean_two)).astype(BF)
            yall[myrows, :] = y_one
            start(send_y, 0, nh)
            slots(ysb1, y_one)
            start(cross_y1, 0, nd)
            ysl[0, myrows, :] = ysb[d]
            arrived(cross_y2, 1, nd)
            for j in range(1, nd):
                ysl[j, myrows, :] = yzr[j]
            start(spread_y, 1, nh)
            arrived(spread_n, 1, nh)
            arrived(cross_hg, 1, nd)
            up_grad()
            arrived(cross_act, 1, nd)
            arrived(spread_y, 1, nh)
            down_grad()
            sent(send_n, 1, nh)
            sent(cross_n, 1, nd)
            sent(cross_act, 1, nd)
            sent(send_p, 1, nh)
            sent(spread_n, 1, nh)
            sent(send_g, 1, nh)
            sent(cross_hg, 1, nd)
            sent(send_d, 1, nh)
            sent(cross_y2, 1, nd)
            sent(send_y, 0, nh)
            sent(cross_y1, 0, nd)
            sent(spread_y, 1, nh)

    return kernel


def solution(mesh):
    nd, nh = mesh.shape["dp"], mesh.shape["head"]

    def per_device(tokens, up, down, neck, casc, clsw, bins, positive, targets):
        rows, width = tokens.shape
        wsl, hid = up.shape[1:]
        levels, chan, cls = clsw.shape
        rois, ksamp = bins.shape
        rb, qb = rows // nh, rois // nh
        labels = jnp.where(positive[:, None] == 1, targets, -1)
        vmem = pltpu.VMEM
        scratch = [
            vmem((nd, wsl, hid), BF), vmem((nd, hid, wsl), BF), vmem((rows, width), BF), vmem((rows, width), BF),
            vmem((rows, hid), F32), vmem((nd, rows, hid), BF), vmem((nd, rows, hid), BF), vmem((rows, width), BF),
            vmem((nh, rb, width), BF), vmem((nh, rb, width), BF), vmem((rows, width), BF),
            vmem((rois, chan), BF), vmem((nh, qb, chan), BF), vmem((rois, chan), BF),
            vmem((rb, width), BF), vmem((nd, rb, wsl), BF), vmem((nd, rb, wsl), BF), vmem((nd, rows, wsl), BF),
            vmem((nd, rb, wsl), BF), vmem((nd, rb, wsl), BF), vmem((nd, rb, wsl), BF), vmem((nd, rows, wsl), BF),
            vmem(neck.shape, BF), vmem(casc.shape, BF), vmem(clsw.shape, BF), vmem((levels, chan, 128), BF), vmem((2 * levels, qb, chan), F32),
            vmem(bins.shape, jnp.int32), vmem(labels.shape, jnp.int32), vmem((rois, rows), BF),
            pltpu.SemaphoreType.DMA((8,)), pltpu.SemaphoreType.DMA((15, 16)), pltpu.SemaphoreType.DMA((15, 16)),
            pltpu.SemaphoreType.REGULAR,
        ]
        kernel = make_kernel(nd, nh, (rows, width, wsl, hid, chan, cls, levels, rois, ksamp))
        return pl.pallas_call(
            kernel,
            out_shape=(
                jax.ShapeDtypeStruct((1, wsl, hid), F32),
                jax.ShapeDtypeStruct((1, hid, wsl), F32),
            ),
            in_specs=[pl.BlockSpec(memory_space=pl.ANY)] * 8,
            out_specs=[pl.BlockSpec(memory_space=vmem)] * 2,
            scratch_shapes=scratch,
            compiler_params=pltpu.CompilerParams(
                collective_id=1, has_side_effects=True, vmem_limit_bytes=56 * 2**20
            ),
            name="window",
        )(tokens, up, down, neck, casc, clsw, bins, labels)

    return jax.shard_map(
        per_device,
        mesh=mesh,
        in_specs=(
            P("dp", None), P("section", "dp", "head"), P("section", "head", "dp"), P(), P(), P(),
            P("dp", None), P("dp"), P("dp", None),
        ),
        out_specs=(P("section", "dp", "head"), P("section", "head", "dp")),
        check_vma=False,
    )
```

time: 1260 us -> 167 us (0.13)
  waiting for transfers between devices: 959 us -> 0 us
  Pallas kernels: 0 us -> 154 us
  blocking collectives: 86 us -> 0 us
  local copies, waits for them, and re-layouts: 77.3 us -> 10.4 us
  matrix products: 64.1 us -> 0 us
  other arithmetic: 45.5 us -> 1.53 us
  between operations: 14.5 us -> 0.65 us
    psum x9 -> x0, waiting for transfers between devices: 813 us -> none  [head_total(): return lax.psum(values, 'head')]
    pallas_call x0 -> x1, Pallas kernels: none -> 154 us  [per_device(): pl.pallas_call(kernel, out_shape=(jax.ShapeDtypeStruct((1, wsl, hid), F32...]
    psum x1 -> x0, blocking collectives: 86 us -> none  [per_device(): lax.psum(transpose_dot(pooling, pooled_grad), 'head').astype(jnp.bfloat16)]
    unnamed x15 -> x0, waiting for transfers between devices: 75.2 us -> none
    all_gather x2 -> x0, waiting for transfers between devices: 66.4 us -> none  [the longest x1 33.8 us: per_device(): lax.all_gather(down_weight, 'dp', axis=2, tiled=True)]
    dot_general x32 -> x0, matrix products: 64.1 us -> none  [the longest x15 31 us: dot_trans(): lax.dot_general(left_side, right_side, (((1,), (1,)), ((), ())), preferre...]
    dynamic_slice x27 -> x0, local copies, waits for them, and re-layouts: 31.2 us -> none  [the longest x23 29.6 us: keep_slot(): old_value = lax.dynamic_index_in_dim(stack_arr, slot_pos, 0, keepdims=False)]
    dynamic_update_slice x16 -> x0, other arithmetic: 24.4 us -> none  [keep_slot(): return lax.dynamic_update_index_in_dim(stack_arr, new_value, slot_pos, 0)]
  transfers between devices with their start and end apart: 21 -> 0, of which waited for: 18 -> 0; matrix products, arithmetic and copies ran while one was open for 6% -> 0% of each run, Pallas kernels for 0% -> 0%
where the time goes in v1:
time: 167 us
  Pallas kernels  154 us (92%)
  local copies, waits for them, and re-layouts  10.4 us (6%)
    pallas_call x1, Pallas kernels, per_device(): pl.pallas_call(kernel, out_shape=(jax.ShapeDtypeStruct((1, wsl, hid), F32...  154 us
    unnamed x6, local copies, waits for them, and re-layouts  10.4 us

profile of v1, /device:TPU:32, one launch (start us, length us, event | category | flops | bytes accessed | tf_op | source)
XLA Modules:
  0.0 166.5 jit_solution(1552662896670628399)
XLA Ops:
  0.6 0.7 broadcast_compare_fusion
  1.3 1.6 copy.14.bins
  2.9 0.8 copy.11
  3.8 0.8 broadcast_select_fusion.labels
  4.6 2.2 %copy.13.clsw = bf16[3,1024,80]{2,1,0:T(8,128)(2,1)} copy(bf16[3,1024,80]{1,2,0:T(8,128)(2,1)} %param.14) | data formatting | bytes 983040 | tf_op args[5]
  6.8 2.2 %copy.12.tokens = bf16[256,1600]{1,0:T(8,128)(2,1)} copy(bf16[256,1600]{0,1:T(8,128)(2,1)} %param.9) | data formatting | bytes 1638400 | tf_op args[0]
  9.0 154.0 %window.1 = (f32[1,200,400]{2,1,0:T(8,128)}, f32[1,400,200]{2,1,0:T(8,128)}) custom-call(bf16[256,1600]{1,0:T(8,128)(2,1)} %copy.12.tokens, bf16[1,200,400]{2,1,0:T(8,128)(2,1)} %up.1, bf16[1,400,200]{2,1,0:T(8,128)(2,1)} %down.1, bf16[1600,1024]{1,0:T(8,128)(2,1)} %neck.1, bf16[3,1024,1024]{2,1,0:T(8,128)(2,1)} %casc.1, bf16[3,1024,80]{2,1,0:T(8,128)(2,1)} %copy.13.clsw, ...), custom_call_target="tpu_custom_call" | custom-call | tf_op jit(solution)/shard_map/window/pallas_call | solution.py:416
  163.0 1.8 %copy.17 = f32[1,200,400]{2,1,0:T(8,128)} copy(f32[1,200,400]{2,1,0:T(8,128)} %get-tuple-element.4) | data formatting | bytes 640000
  164.8 1.8 %copy.18 = f32[1,400,200]{2,1,0:T(8,128)} copy(f32[1,400,200]{2,1,0:T(8,128)} %get-tuple-element.5) | data formatting | bytes 640000

commit v2 on v1

v2 whole, which is shorter than its diff:
```python
import jax
import jax.numpy as jnp
from jax import lax
from jax.experimental import pallas as pl
from jax.experimental.pallas import tpu as pltpu
from jax.sharding import PartitionSpec as P

MESH = pl.DeviceIdType.MESH
EPS = 1e-06
BF = jnp.bfloat16
F32 = jnp.float32


def dot(a, b):
    return jnp.dot(a, b, preferred_element_type=F32)


def dot_rt(a, b):
    return lax.dot_general(a, b, (((1,), (1,)), ((), ())), preferred_element_type=F32)


def dot_lt(a, b):
    return lax.dot_general(a, b, (((0,), (0,)), ((), ())), preferred_element_type=F32)


def gelu_both(z):
    c = 0.7978845608028654
    zz = z * z
    t = jnp.tanh(c * z * (1.0 + 0.044715 * zz))
    half = 0.5 * (1.0 + t)
    slope = half + (0.5 * c) * z * (1.0 - t * t) * (1.0 + (3 * 0.044715) * zz)
    return z * half, slope


def norm_rows(x):
    centre = x - jnp.mean(x, axis=-1, keepdims=True)
    inv = lax.rsqrt(jnp.mean(centre * centre, axis=-1, keepdims=True) + EPS)
    return centre * inv, inv


def row_cuts(total, pieces):
    tiles = total // 16
    edges = [16 * (tiles * p // pieces) for p in range(pieces)] + [total]
    return [(a, b - a) for a, b in zip(edges, edges[1:])]


def hand_over(up_in, down_in, up_out, down_out):
    up_out[...] = up_in[...]
    down_out[...] = down_in[...]


def make_kernel(nd, nh, dims):
    rows, width, wsl, hid, chan, cls, levels, rois, ksamp = dims
    rb = rows // nh
    qb = rois // nh
    side = int(round(nh**0.5))
    n_right = nd // 2
    n_left = nd - 1 - n_right

    def kernel(
        tokens, up, down, neck, casc, clsw, bins, positive, targets, gup, gdn,
        upg, dng, xt, xb, nrm, slope, act, hg, part, rs_a, rs_d, yall, feat, ppart, prec, pg,
        xrow, yrow, nsb, nzr, nsl, ysb, ysb1, yzr, ysl, neckv, cascv, casct, clsr, clsv, clst, terms,
        binv, posv, tarv, hits, poolv, poolt, wv, wl, wt, wlt, lsem, ss, rs, ring_ss, ring_rs, zgo,
    ):
        s = lax.axis_index("section")
        d = lax.axis_index("dp")
        h = lax.axis_index("head")
        myrows = pl.ds(pl.multiple_of(h * rb, rb), rb)
        myrois = pl.ds(pl.multiple_of(h * qb, qb), qb)

        def loop(a, b, body):
            def step(k, c):
                body(k)
                return c

            lax.fori_loop(a, b, step, 0)

        far_plane = sorted(range(nh), key=lambda k: -sum(min(o, side - o) for o in (k // side, k % side)))
        far_column = sorted(range(nd), key=lambda k: -min(k, nd - k))

        def partner(k):
            return lax.rem(h // side + k // side, side) * side + lax.rem(h + k % side, side)

        def plane(row, src, dst, core):
            def make(k):
                t = partner(k)
                return pltpu.make_async_remote_copy(
                    src_ref=src(t), dst_ref=dst(k), send_sem=ss.at[row, k], recv_sem=rs.at[row, k],
                    device_id=(core, d, t), device_id_type=MESH,
                )

            return make

        def column(row, src, dst, core):
            def make(k):
                t = lax.rem(d + k, nd)
                return pltpu.make_async_remote_copy(
                    src_ref=src(t), dst_ref=dst(k), send_sem=ss.at[row, k], recv_sem=rs.at[row, k],
                    device_id=(core, t, h), device_id_type=MESH,
                )

            return make

        def ring(row, buf, relative, rights, lefts, cuts):
            def slot(j):
                return j if relative else lax.rem(d - j + nd, nd)

            def copy(src, dst, piece, to):
                return pltpu.make_async_remote_copy(
                    src_ref=buf.at[(slot(src), *cuts[piece])],
                    dst_ref=buf.at[(dst if relative else slot(src), *cuts[piece])],
                    send_sem=ring_ss.at[row, dst, piece], recv_sem=ring_rs.at[row, dst, piece],
                    device_id=(s, lax.rem(d + to, nd), h), device_id_type=MESH,
                )

            def right(t, piece):
                return copy(t, t + 1, piece, 1)

            def left(t, piece):
                return copy((nd - t) % nd, nd - 1 - t, piece, nd - 1)

            return [(right, rights, len(cuts)), (left, lefts, len(cuts))]

        def ring_step(chains, t):
            for piece in range(max(pieces for _, _, pieces in chains)):
                for make, count, pieces in chains:
                    if t < count and piece < pieces:
                        if t > 0:
                            make(t - 1, piece).wait_recv()
                        make(t, piece).start()

        def ring_last(chains):
            for make, count, pieces in chains:
                for piece in range(pieces):
                    make(count - 1, piece).wait_recv()

        def ring_sent(chains):
            for make, count, pieces in chains:
                for t in range(count):
                    for piece in range(pieces):
                        make(t, piece).wait_send()

        load_up = pltpu.make_async_copy(up.at[0], upg.at[d], lsem.at[0])
        load_down = pltpu.make_async_copy(down.at[0], dng.at[d], lsem.at[1])
        load_up.start()
        load_down.start()
        barrier = pltpu.get_barrier_semaphore()

        def greet_plane(k):
            pl.semaphore_signal(barrier, inc=1, device_id=(s, d, partner(k)), device_id_type=MESH)

        def greet_plane_other(k):
            pl.semaphore_signal(barrier, inc=1, device_id=(1 - s, d, partner(k)), device_id_type=MESH)

        def greet_column(k):
            pl.semaphore_signal(barrier, inc=1, device_id=(s, lax.rem(d + k, nd), h), device_id_type=MESH)
            pl.semaphore_signal(barrier, inc=1, device_id=(1 - s, lax.rem(d + k, nd), h), device_id_type=MESH)

        loop(1, nd, greet_column)
        loop(1, nh, greet_plane)
        loop(0, nh, greet_plane_other)

        load_tok = pltpu.make_async_copy(tokens, xt, lsem.at[2])
        load_neck = pltpu.make_async_copy(neck, neckv, lsem.at[3])
        load_casc = pltpu.make_async_copy(casc, cascv, lsem.at[4])
        load_cls = pltpu.make_async_copy(clsw, clsr, lsem.at[5])
        load_bins = pltpu.make_async_copy(bins, binv, lsem.at[6])
        load_pos = pltpu.make_async_copy(positive, posv, lsem.at[7])
        load_tar = pltpu.make_async_copy(targets, tarv, lsem.at[8])
        load_tok.start()

        @pl.when(s == 1)
        def _():
            for c in (load_bins, load_pos, load_tar, load_neck, load_casc, load_cls):
                c.start()

        load_up.wait()
        load_down.wait()
        pl.semaphore_wait(barrier, 2 * (nd - 1) + 2 * nh - 1)

        all_of = slice(None)
        up_cuts = [(all_of, slice(a, min(a + 128, hid))) for a in range(0, hid, 128)]
        down_cuts = [(pl.ds(a, n),) for a, n in row_cuts(hid, 4)]
        hg_cuts = [(pl.ds(a, n),) for a, n in row_cuts(rows, 4)]
        chains = ring(0, upg, False, n_right, n_left, up_cuts) + ring(1, dng, False, n_left, n_right, down_cuts)

        send_a = plane(2, lambda t: part.at[pl.ds(pl.multiple_of(t * rb, rb), rb)], lambda k: rs_a.at[k], 1)
        send_n = plane(3, lambda t: nrm.at[myrows], lambda k: nrm.at[myrows], 1)
        send_p = plane(4, lambda t: ppart.at[pl.ds(pl.multiple_of(t * qb, qb), qb)], lambda k: prec.at[k], 1)
        send_g = plane(5, lambda t: pg.at[myrois], lambda k: pg.at[myrois], 1)
        send_d = plane(6, lambda t: part.at[pl.ds(pl.multiple_of(t * rb, rb), rb)], lambda k: rs_d.at[k], 1)
        send_y = plane(7, lambda t: yall.at[myrows], lambda k: yall.at[myrows], 0)
        spread_n = plane(8, lambda t: nsl.at[:, myrows, :], lambda k: nsl.at[:, myrows, :], s)
        spread_y = plane(9, lambda t: ysl.at[:, myrows, :], lambda k: ysl.at[:, myrows, :], s)
        cross_n = column(10, lambda t: nsb.at[t], lambda k: nzr.at[k], s)
        cross_y2 = column(11, lambda t: ysb.at[t], lambda k: yzr.at[k], 1)
        cross_y1 = column(14, lambda t: ysb1.at[t], lambda k: yzr.at[k], 0)
        hg_ring = ring(2, hg, True, n_right, n_left, hg_cuts)
        act_ring = ring(3, act, True, n_left, n_right, hg_cuts)

        def start(make, a, b):
            order = far_plane if b == nh else far_column
            for k in order:
                if k >= a:
                    make(k).start()

        def arrived(make, a, b):
            loop(a, b, lambda k: make(k).wait_recv())

        def sent(make, a, b):
            loop(a, b, lambda k: make(k).wait_send())

        def lanes(j):
            return slice(j * wsl, (j + 1) * wsl)

        def forward():
            before = dot(nrm[:, lanes(0)], upg[0])
            for j in range(1, nd):
                before = before + dot(nrm[:, lanes(j)], upg[j])
            value, rise = gelu_both(before)
            slope[...] = rise
            act[0] = value.astype(BF)

        def down_sum():
            active = act[0]
            for j in range(nd):
                part[:, lanes(j)] = dot(active, dng[j]).astype(BF)

        def backward():
            grad = dot_rt(yall[:, lanes(0)], dng[0])
            for j in range(1, nd):
                grad = grad + dot_rt(yall[:, lanes(j)], dng[j])
            hg[0] = (grad * slope[...]).astype(BF)

        def slots(dst, values):
            for j in range(nd):
                dst[j] = values[:, lanes(j)]

        def up_grad(j):
            term = dot_lt(nsl[j], hg[j])
            gup[0] = term if j == 0 else gup[0] + term

        def down_grad():
            total = dot_lt(act[0], ysl[0])
            for j in range(1, nd):
                total = total + dot_lt(act[j], ysl[j])
            gdn[0] = total

        @pl.when(s == 0)
        def _():
            ring_step(chains, 0)
            load_tok.wait()
            xb[...] = xt[...].T
            nrm[...] = norm_rows(xb[...].astype(F32))[0].astype(BF)
            slots(nsb, nrm[myrows, :])
            for t in range(1, n_right):
                ring_step(chains, t)
            pl.semaphore_signal(zgo, inc=1, device_id=(1, d, h), device_id_type=MESH)
            ring_last(chains)
            forward()
            down_sum()
            start(send_a, 0, nh)
            start(cross_n, 1, nd)
            nsl[0, myrows, :] = nsb[d]
            pl.semaphore_wait(zgo, 1)
            ring_step(act_ring, 0)
            arrived(cross_n, 1, nd)
            for j in range(1, nd):
                nsl[j, myrows, :] = nzr[j]
            sent(send_a, 0, nh)
            for t in range(1, n_right):
                ring_step(act_ring, t)
            ring_last(act_ring)
            start(spread_n, 1, nh)
            arrived(spread_n, 1, nh)
            ring_sent(chains)
            ring_sent(act_ring)
            sent(cross_n, 1, nd)
            sent(spread_n, 1, nh)
            arrived(send_y, 0, nh)
            backward()
            ring_step(hg_ring, 0)
            arrived(cross_y1, 0, nd)
            for j in range(nd):
                ysl[j, myrows, :] = yzr[j]
            start(spread_y, 1, nh)
            up_grad(0)
            for t in range(1, n_right):
                ring_step(hg_ring, t)
                if t == 2:
                    arrived(spread_y, 1, nh)
                    down_grad()
                up_grad(t)
                if t < n_left:
                    up_grad(nd - t)
            ring_last(hg_ring)
            for t in range(n_right, nd - n_left + 1):
                up_grad(t)
            ring_sent(hg_ring)
            sent(spread_y, 1, nh)

        @pl.when(s == 1)
        def _():
            load_bins.wait()
            spots = lax.broadcasted_iota(jnp.int32, (rows, rois), 0)
            found = binv[...]
            count = jnp.zeros((rows, rois), F32)
            for j in range(ksamp):
                count = count + jnp.where(found[j : j + 1, :] == spots, 1.0, 0.0)
            poolt[...] = (count * (1.0 / ksamp)).astype(BF)
            poolv[...] = (count * (1.0 / ksamp)).T.astype(BF)
            load_pos.wait()
            load_tar.wait()
            classes = lax.broadcasted_iota(jnp.int32, (128, rois), 0)
            for j in range(levels):
                wanted = (tarv[j : j + 1, :] == classes) & (posv[...] == 1)
                hits[j] = jnp.where(wanted, 1.0, 0.0).T
            load_tok.wait()
            xb[...] = xt[...].T
            load_cls.wait()
            clsv[...] = jnp.zeros(clsv.shape, BF)
            clsv[:, 0:cls, :] = clsr[...]
            load_casc.wait()
            for j in range(levels):
                clst[j] = clsv[j].T
                casct[j] = cascv[j].T
            load_neck.wait()
            pl.semaphore_wait(zgo, 1)
            for t in range(n_right):
                ring_step(chains, t)
            ring_last(chains)
            pl.semaphore_signal(zgo, inc=1, device_id=(0, d, h), device_id_type=MESH)

            total = xb[myrows, :].astype(F32)
            arrived(send_a, 0, nh)
            for k in range(nh):
                total = total + rs_a[k].astype(F32)
            xrow[...] = total.astype(BF)
            normed = norm_rows(xrow[...].astype(F32))[0].astype(BF)
            nrm[myrows, :] = normed
            start(send_n, 1, nh)
            slots(nsb, normed)
            start(cross_n, 1, nd)
            both = dot(dng[0], neckv[0])
            kept = dot(xrow[:, lanes(0)], neckv[0])
            for j in range(1, nd):
                both = both + dot(dng[j], neckv[j])
                kept = kept + dot(xrow[:, lanes(j)], neckv[j])
            wv[...] = both.astype(BF)
            wl[...] = (both - wv[...].astype(F32)).astype(BF)
            arrived(send_n, 1, nh)
            forward()
            feat[...] = dot(act[0], wv[...]).astype(BF)
            feat[myrows, :] = (feat[myrows, :].astype(F32) + kept).astype(BF)
            ppart[...] = dot(poolv[...], feat[...]).astype(BF)
            start(send_p, 1, nh)
            ring_step(act_ring, 0)
            wt[...] = wv[...].T
            wlt[...] = wl[...].T
            nsl[0, myrows, :] = nsb[d]
            arrived(cross_n, 1, nd)
            for j in range(1, nd):
                nsl[j, myrows, :] = nzr[j]
            total = ppart[myrois, :].astype(F32)
            arrived(send_p, 1, nh)
            for k in range(1, nh):
                total = total + prec[k].astype(F32)

            ring_step(act_ring, 1)
            start(spread_n, 1, nh)

            current = total.astype(BF)
            lane = lax.broadcasted_iota(jnp.int32, (qb, 128), 1)
            rises = []
            for j in range(levels):
                value, rise = gelu_both(dot(current, cascv[j]))
                rises.append(rise)
                current = (current.astype(F32) + value).astype(BF)
                error = jax.nn.sigmoid(dot(current, clst[j])) - hits[j, myrois, :]
                error = jnp.where(lane < cls, error, 0.0).astype(BF)
                terms[2 * j] = dot(error, clsv[j])
            running = jnp.zeros((qb, chan), F32)
            for j in reversed(range(levels)):
                running = running + terms[2 * j]
                through = (running * rises[j]).astype(BF)
                terms[2 * j + 1] = dot(through, casct[j])
                running = running + terms[2 * j + 1]
            pg[myrois, :] = running.astype(BF)
            start(send_g, 1, nh)
            ring_step(act_ring, 2)
            ring_step(act_ring, 3)
            ring_last(act_ring)
            arrived(send_g, 1, nh)

            feat[...] = dot(poolt[...], pg[...]).astype(BF)
            grad = dot(feat[...], wt[...]) + dot(feat[...], wlt[...])
            hg[0] = (grad * slope[...]).astype(BF)
            ring_step(hg_ring, 0)
            hidden = hg[0]
            for j in range(nd):
                part[:, lanes(j)] = dot_rt(hidden, upg[j]).astype(BF)
            start(send_d, 1, nh)
            mine = feat[myrows, :]
            for j in range(nd):
                piece = dot_rt(mine, neckv[j]).astype(BF)
                ysb[j] = piece
                yrow[:, lanes(j)] = piece
            start(cross_y2, 1, nd)
            scaled, inv = norm_rows(xrow[...].astype(F32))
            total = part[myrows, :].astype(F32)
            ring_step(hg_ring, 1)
            arrived(send_d, 1, nh)
            for k in range(1, nh):
                total = total + rs_d[k].astype(F32)
            mean_one = jnp.mean(total, axis=-1, keepdims=True)
            mean_two = jnp.mean(total * scaled, axis=-1, keepdims=True)
            y_one = (yrow[...].astype(F32) + inv * (total - mean_one - scaled * mean_two)).astype(BF)
            yall[myrows, :] = y_one
            start(send_y, 0, nh)
            slots(ysb1, y_one)
            start(cross_y1, 0, nd)
            ring_step(hg_ring, 2)
            ysl[0, myrows, :] = ysb[d]
            arrived(cross_y2, 1, nd)
            for j in range(1, nd):
                ysl[j, myrows, :] = yzr[j]
            start(spread_y, 1, nh)
            arrived(spread_n, 1, nh)
            ring_step(hg_ring, 3)
            ring_last(hg_ring)
            for j in range(nd):
                up_grad(j)
            arrived(spread_y, 1, nh)
            down_grad()
            sent(send_n, 1, nh)
            sent(cross_n, 1, nd)
            ring_sent(act_ring)
            sent(send_p, 1, nh)
            sent(spread_n, 1, nh)
            sent(send_g, 1, nh)
            ring_sent(chains)
            ring_sent(hg_ring)
            sent(send_d, 1, nh)
            sent(cross_y2, 1, nd)
            sent(send_y, 0, nh)
            sent(cross_y1, 0, nd)
            sent(spread_y, 1, nh)

    return kernel


def solution(mesh):
    nd, nh = mesh.shape["dp"], mesh.shape["head"]

    def per_device(tokens, up, down, neck, casc, clsw, bins, positive, targets):
        rows, width = tokens.shape
        wsl, hid = up.shape[1:]
        levels, chan, cls = clsw.shape
        rois, ksamp = bins.shape
        rb, qb = rows // nh, rois // nh
        vmem = pltpu.VMEM
        scratch = [
            vmem((nd, wsl, hid), BF), vmem((nd, hid, wsl), BF), vmem((width, rows), BF),
            vmem((rows, width), BF), vmem((rows, width), BF),
            vmem((rows, hid), F32), vmem((nd, rows, hid), BF), vmem((nd, rows, hid), BF), vmem((rows, width), BF),
            vmem((nh, rb, width), BF), vmem((nh, rb, width), BF), vmem((rows, width), BF), vmem((rows, chan), BF),
            vmem((rois, chan), BF), vmem((nh, qb, chan), BF), vmem((rois, chan), BF),
            vmem((rb, width), BF), vmem((rb, width), BF),
            vmem((nd, rb, wsl), BF), vmem((nd, rb, wsl), BF), vmem((nd, rows, wsl), BF),
            vmem((nd, rb, wsl), BF), vmem((nd, rb, wsl), BF), vmem((nd, rb, wsl), BF), vmem((nd, rows, wsl), BF),
            vmem((nd, wsl, chan), BF), vmem(casc.shape, BF), vmem(casc.shape, BF),
            vmem((levels, cls, chan), BF), vmem((levels, 128, chan), BF), vmem((levels, chan, 128), BF),
            vmem((2 * levels, qb, chan), F32),
            vmem((ksamp, rois), jnp.int32), vmem((1, rois), jnp.int32), vmem((levels, rois), jnp.int32),
            vmem((levels, rois, 128), F32), vmem((rois, rows), BF), vmem((rows, rois), BF),
            vmem((hid, chan), BF), vmem((hid, chan), BF), vmem((chan, hid), BF), vmem((chan, hid), BF),
            pltpu.SemaphoreType.DMA((9,)), pltpu.SemaphoreType.DMA((15, 16)), pltpu.SemaphoreType.DMA((15, 16)),
            pltpu.SemaphoreType.DMA((4, nd, 4)), pltpu.SemaphoreType.DMA((4, nd, 4)),
            pltpu.SemaphoreType.REGULAR,
        ]
        kernel = make_kernel(nd, nh, (rows, width, wsl, hid, chan, cls, levels, rois, ksamp))
        results = pl.pallas_call(
            kernel,
            out_shape=(
                jax.ShapeDtypeStruct((1, wsl, hid), F32),
                jax.ShapeDtypeStruct((1, hid, wsl), F32),
            ),
            in_specs=[pl.BlockSpec(memory_space=pl.ANY)] * 9,
            out_specs=[pl.BlockSpec(memory_space=vmem)] * 2,
            scratch_shapes=scratch,
            compiler_params=pltpu.CompilerParams(
                collective_id=1, has_side_effects=True, vmem_limit_bytes=56 * 2**20
            ),
            name="window",
        )(
            tokens.T, up, down, neck.reshape(nd, wsl, chan), casc, clsw.transpose(0, 2, 1), bins.T,
            positive.reshape(1, rois), targets.T,
        )
        return pl.pallas_call(
            hand_over,
            out_shape=tuple(jax.ShapeDtypeStruct(r.shape, r.dtype) for r in results),
            in_specs=[pl.BlockSpec(memory_space=vmem)] * 2,
            out_specs=[pl.BlockSpec(memory_space=vmem)] * 2,
            name="hand_over",
        )(*results)

    return jax.shard_map(
        per_device,
        mesh=mesh,
        in_specs=(
            P("dp", None), P("section", "dp", "head"), P("section", "head", "dp"), P(), P(), P(),
            P("dp", None), P("dp"), P("dp", None),
        ),
        out_specs=(P("section", "dp", "head"), P("section", "head", "dp")),
        check_vma=False,
    )
```

time: 167 us -> 128 us (0.77)
  Pallas kernels: 154 us -> 126 us
  local copies, waits for them, and re-layouts: 10.4 us -> 0 us
    pallas_call x1, Pallas kernels: 154 us -> 124 us  [per_device(): pl.pallas_call(kernel, out_shape=(jax.ShapeDtypeStruct((1, wsl, hid), F32...]
    unnamed x6 -> x0, local copies, waits for them, and re-layouts: 10.4 us -> none
    pallas_call x0 -> x1, Pallas kernels: none -> 2.04 us  [per_device(): pl.pallas_call(hand_over, out_shape=tuple((jax.ShapeDtypeStruct(r.shape,...]
where the time goes in v2:
time: 128 us; the launch traced here: 127 us
  Pallas kernels  126 us (98%)
    pallas_call x1, Pallas kernels, per_device(): pl.pallas_call(kernel, out_shape=(jax.ShapeDtypeStruct((1, wsl, hid), F32...  124 us

profile of v2, /device:TPU:32, one launch (start us, length us, event | category | flops | bytes accessed | tf_op | source)
XLA Modules:
  0.0 126.7 jit_solution(9088041383566088263)
XLA Ops:
  0.6 124.0 %window.1 = (f32[1,200,400]{2,1,0:T(8,128)}, f32[1,400,200]{2,1,0:T(8,128)}) custom-call(bf16[1600,256]{1,0:T(8,128)(2,1)} %bitcast.7, bf16[1,200,400]{2,1,0:T(8,128)(2,1)} %up.1, bf16[1,400,200]{2,1,0:T(8,128)(2,1)} %down.1, bf16[8,200,1024]{2,1,0:T(8,128)(2,1)} %bitcast.6, bf16[3,1024,1024]{2,1,0:T(8,128)(2,1)} %casc.1, bf16[3,80,1024]{2,1,0:T(8,128)(2,1)} %bitcast.8, ...), custom_call_target="tpu_custom_call" | custom-call | tf_op jit(solution)/shard_map/window/pallas_call | solution.py:483
  124.7 2.0 %hand_over.1 = (f32[1,200,400]{2,1,0:T(8,128)}, f32[1,400,200]{2,1,0:T(8,128)}) custom-call(f32[1,200,400]{2,1,0:T(8,128)} %get-tuple-element.4.up_in, f32[1,400,200]{2,1,0:T(8,128)} %get-tuple-element.5.down_in), custom_call_target="tpu_custom_call" | custom-call | tf_op jit(solution)/shard_map/hand_over/pallas_call | solution.py:500

commit v3 on v2

--- a/solution.py
+++ b/solution.py
@@ -54,15 +54,19 @@
     rb = rows // nh
     qb = rois // nh
     side = int(round(nh**0.5))
+    body = hid // 128 * 128
+    rest = hid - body
+    packed = rows + 16
     n_right = nd // 2
     n_left = nd - 1 - n_right
 
     def kernel(
         tokens, up, down, neck, casc, clsw, bins, positive, targets, gup, gdn,
-        upg, dng, xt, xb, nrm, slope, act, hg, part, rs_a, rs_d, yall, feat, ppart, prec, pg,
+        wg, dtg, upr, downr, xt, xb, nrm, slope, act, hg, last, part, rs_a, rs_d, yall, feat, ppart, prec, pg,
         xrow, yrow, nsb, nzr, nsl, ysb, ysb1, yzr, ysl, neckv, cascv, casct, clsr, clsv, clst, terms,
-        binv, posv, tarv, hits, poolv, poolt, wv, wl, wt, wlt, lsem, ss, rs, ring_ss, ring_rs, zgo,
+        binv, posv, tarv, hits, poolv, poolt, wv, wl, wt, wlt, lsem, ss, rs, ring_ss, ring_w, ring_h, ring_a, zgo,
     ):
+        ring_rs = (ring_w, ring_h, ring_a)
         s = lax.axis_index("section")
         d = lax.axis_index("dp")
         h = lax.axis_index("head")
@@ -82,27 +86,34 @@
         def partner(k):
             return lax.rem(h // side + k // side, side) * side + lax.rem(h + k % side, side)
 
-        def plane(row, src, dst, core):
+        def exchange(row, src, dst, place, whole_src, whole_dst):
             def make(k):
-                t = partner(k)
                 return pltpu.make_async_remote_copy(
-                    src_ref=src(t), dst_ref=dst(k), send_sem=ss.at[row, k], recv_sem=rs.at[row, k],
-                    device_id=(core, d, t), device_id_type=MESH,
+                    src_ref=src(k), dst_ref=dst(k), send_sem=ss.at[row], recv_sem=rs.at[row],
+                    device_id=place(k), device_id_type=MESH,
                 )
 
-            return make
-
-        def column(row, src, dst, core):
-            def make(k):
-                t = lax.rem(d + k, nd)
+            def whole():
                 return pltpu.make_async_remote_copy(
-                    src_ref=src(t), dst_ref=dst(k), send_sem=ss.at[row, k], recv_sem=rs.at[row, k],
-                    device_id=(core, t, h), device_id_type=MESH,
+                    src_ref=whole_src, dst_ref=whole_dst, send_sem=ss.at[row], recv_sem=rs.at[row],
+                    device_id=place(1), device_id_type=MESH,
                 )
 
-            return make
-
-        def ring(row, buf, relative, rights, lefts, cuts):
+            return make, whole
+
+        def plane(row, src, dst, core, whole_src, whole_dst):
+            def place(k):
+                return (core, d, partner(k))
+
+            return exchange(row, lambda k: src(partner(k)), dst, place, whole_src, whole_dst)
+
+        def column(row, src, dst, core, whole_src, whole_dst):
+            def place(k):
+                return (core, lax.rem(d + k, nd), h)
+
+            return exchange(row, lambda k: src(lax.rem(d + k, nd)), dst, place, whole_src, whole_dst)
+
+        def ring(row, buf, relative, rights, lefts, cuts, whole):
             def slot(j):
                 return j if relative else lax.rem(d - j + nd, nd)
 
@@ -110,7 +121,7 @@
                 return pltpu.make_async_remote_copy(
                     src_ref=buf.at[(slot(src), *cuts[piece])],
                     dst_ref=buf.at[(dst if relative else slot(src), *cuts[piece])],
-                    send_sem=ring_ss.at[row, dst, piece], recv_sem=ring_rs.at[row, dst, piece],
+                    send_sem=ring_ss.at[row], recv_sem=ring_rs[row].at[dst - 1, piece],
                     device_id=(s, lax.rem(d + to, nd), h), device_id_type=MESH,
                 )
 
@@ -120,29 +131,32 @@
             def left(t, piece):
                 return copy((nd - t) % nd, nd - 1 - t, piece, nd - 1)
 
-            return [(right, rights, len(cuts)), (left, lefts, len(cuts))]
+            def all_sent():
+                pltpu.make_async_remote_copy(
+                    src_ref=whole, dst_ref=whole, send_sem=ring_ss.at[row], recv_sem=ring_rs[row].at[0, 0],
+                    device_id=(s, lax.rem(d + 1, nd), h), device_id_type=MESH,
+                ).wait_send()
+
+            return [(right, rights, len(cuts), all_sent), (left, lefts, len(cuts), all_sent)]
 
         def ring_step(chains, t):
-            for piece in range(max(pieces for _, _, pieces in chains)):
-                for make, count, pieces in chains:
+            for piece in range(max(c[2] for c in chains)):
+                for make, count, pieces, _ in chains:
                     if t < count and piece < pieces:
                         if t > 0:
                             make(t - 1, piece).wait_recv()
                         make(t, piece).start()
 
         def ring_last(chains):
-            for make, count, pieces in chains:
+            for make, count, pieces, _ in chains:
                 for piece in range(pieces):
                     make(count - 1, piece).wait_recv()
 
         def ring_sent(chains):
-            for make, count, pieces in chains:
-                for t in range(count):
-                    for piece in range(pieces):
-                        make(t, piece).wait_send()
-
-        load_up = pltpu.make_async_copy(up.at[0], upg.at[d], lsem.at[0])
-        load_down = pltpu.make_async_copy(down.at[0], dng.at[d], lsem.at[1])
+            chains[0][3]()
+
+        load_up = pltpu.make_async_copy(up.at[0], upr, lsem.at[0])
+        load_down = pltpu.make_async_copy(down.at[0], downr, lsem.at[1])
         load_up.start()
         load_down.start()
         barrier = pltpu.get_barrier_semaphore()
@@ -176,48 +190,69 @@
                 c.start()
 
         load_up.wait()
+        wg[d, :, 0:hid] = upr[...]
         load_down.wait()
+        wg[d, :, hid : 2 * hid] = downr[...].T
         pl.semaphore_wait(barrier, 2 * (nd - 1) + 2 * nh - 1)
 
         all_of = slice(None)
-        up_cuts = [(all_of, slice(a, min(a + 128, hid))) for a in range(0, hid, 128)]
-        down_cuts = [(pl.ds(a, n),) for a, n in row_cuts(hid, 4)]
-        hg_cuts = [(pl.ds(a, n),) for a, n in row_cuts(rows, 4)]
-        chains = ring(0, upg, False, n_right, n_left, up_cuts) + ring(1, dng, False, n_left, n_right, down_cuts)
-
-        send_a = plane(2, lambda t: part.at[pl.ds(pl.multiple_of(t * rb, rb), rb)], lambda k: rs_a.at[k], 1)
-        send_n = plane(3, lambda t: nrm.at[myrows], lambda k: nrm.at[myrows], 1)
-        send_p = plane(4, lambda t: ppart.at[pl.ds(pl.multiple_of(t * qb, qb), qb)], lambda k: prec.at[k], 1)
-        send_g = plane(5, lambda t: pg.at[myrois], lambda k: pg.at[myrois], 1)
-        send_d = plane(6, lambda t: part.at[pl.ds(pl.multiple_of(t * rb, rb), rb)], lambda k: rs_d.at[k], 1)
-        send_y = plane(7, lambda t: yall.at[myrows], lambda k: yall.at[myrows], 0)
-        spread_n = plane(8, lambda t: nsl.at[:, myrows, :], lambda k: nsl.at[:, myrows, :], s)
-        spread_y = plane(9, lambda t: ysl.at[:, myrows, :], lambda k: ysl.at[:, myrows, :], s)
-        cross_n = column(10, lambda t: nsb.at[t], lambda k: nzr.at[k], s)
-        cross_y2 = column(11, lambda t: ysb.at[t], lambda k: yzr.at[k], 1)
-        cross_y1 = column(14, lambda t: ysb1.at[t], lambda k: yzr.at[k], 0)
-        hg_ring = ring(2, hg, True, n_right, n_left, hg_cuts)
-        act_ring = ring(3, act, True, n_left, n_right, hg_cuts)
-
-        def start(make, a, b):
+        mid = 4 * 128
+        w_cuts = [(all_of, slice(0, 256)), (all_of, slice(256, mid)), (all_of, slice(mid, 2 * hid))]
+        hg_cuts = [(pl.ds(a, n),) for a, n in row_cuts(packed, 4)]
+        act_cuts = [(pl.ds(a, n),) for a, n in row_cuts(rows, 2)]
+        chains = ring(0, wg, False, n_right, n_left, w_cuts, wg.at[pl.ds(0, nd - 1)])
+
+        most = rows - rb
+        others = pl.ds(0, most)
+        send_a = plane(0, lambda t: part.at[pl.ds(pl.multiple_of(t * rb, rb), rb)], lambda k: rs_a.at[k], 1, part, rs_a)
+        send_n = plane(1, lambda t: nrm.at[myrows], lambda k: nrm.at[myrows], 1, nrm.at[others], nrm.at[others])
+        send_p = plane(
+            2, lambda t: ppart.at[pl.ds(pl.multiple_of(t * qb, qb), qb)], lambda k: prec.at[k], 1,
+            ppart.at[pl.ds(0, rois - qb)], prec.at[pl.ds(0, nh - 1)],
+        )
+        send_g = plane(
+            3, lambda t: pg.at[myrois], lambda k: pg.at[myrois], 1,
+            pg.at[pl.ds(0, rois - qb)], pg.at[pl.ds(0, rois - qb)],
+        )
+        send_d = plane(
+            4, lambda t: part.at[pl.ds(pl.multiple_of(t * rb, rb), rb)], lambda k: rs_d.at[k], 1,
+            part.at[others], rs_d.at[pl.ds(0, nh - 1)],
+        )
+        send_y = plane(5, lambda t: yall.at[myrows], lambda k: yall.at[myrows], 0, yall, yall)
+        spread_n = plane(
+            6, lambda t: nsl.at[:, myrows, :], lambda k: nsl.at[:, myrows, :], s,
+            nsl.at[:, others, :], nsl.at[:, others, :],
+        )
+        spread_y = plane(
+            7, lambda t: ysl.at[:, myrows, :], lambda k: ysl.at[:, myrows, :], s,
+            ysl.at[:, others, :], ysl.at[:, others, :],
+        )
+        few = pl.ds(0, nd - 1)
+        cross_n = column(8, lambda t: nsb.at[t], lambda k: nzr.at[k], s, nsb.at[few], nzr.at[few])
+        cross_y2 = column(9, lambda t: ysb.at[t], lambda k: yzr.at[k], 1, ysb.at[few], yzr.at[few])
+        cross_y1 = column(10, lambda t: ysb1.at[t], lambda k: yzr.at[k], 0, ysb1, yzr)
+        hg_ring = ring(1, hg, True, n_right, n_left, hg_cuts, hg.at[few])
+        act_ring = ring(2, act, True, n_left, n_right, act_cuts, act.at[few])
+
+        def start(transfer, a, b):
             order = far_plane if b == nh else far_column
             for k in order:
                 if k >= a:
-                    make(k).start()
-
-        def arrived(make, a, b):
-            loop(a, b, lambda k: make(k).wait_recv())
-
-        def sent(make, a, b):
-            loop(a, b, lambda k: make(k).wait_send())
+                    transfer[0](k).start()
+
+        def arrived(transfer):
+            transfer[1]().wait_recv()
+
+        def sent(transfer):
+            transfer[1]().wait_send()
 
         def lanes(j):
             return slice(j * wsl, (j + 1) * wsl)
 
         def forward():
-            before = dot(nrm[:, lanes(0)], upg[0])
-            for j in range(1, nd):
-                before = before + dot(nrm[:, lanes(j)], upg[j])
+            before = dot(nrm[:, lanes(0)], wg[0, :, 0:hid])
+            for j in range(1, nd):
+                before = before + dot(nrm[:, lanes(j)], wg[j, :, 0:hid])
             value, rise = gelu_both(before)
             slope[...] = rise
             act[0] = value.astype(BF)
@@ -225,21 +260,30 @@
         def down_sum():
             active = act[0]
             for j in range(nd):
-                part[:, lanes(j)] = dot(active, dng[j]).astype(BF)
+                part[:, lanes(j)] = dot_rt(active, dtg[j]).astype(BF)
+
+        def keep_hidden(values):
+            hg[0, 0:rows, :] = values[:, 0:body]
+            for r in range(rows // 16):
+                hg[0, rows:packed, r * rest : (r + 1) * rest] = values[16 * r : 16 * r + 16, body:hid]
 
         def backward():
-            grad = dot_rt(yall[:, lanes(0)], dng[0])
-            for j in range(1, nd):
-                grad = grad + dot_rt(yall[:, lanes(j)], dng[j])
-            hg[0] = (grad * slope[...]).astype(BF)
+            grad = dot(yall[:, lanes(0)], dtg[0])
+            for j in range(1, nd):
+                grad = grad + dot(yall[:, lanes(j)], dtg[j])
+            keep_hidden((grad * slope[...]).astype(BF))
 
         def slots(dst, values):
             for j in range(nd):
                 dst[j] = values[:, lanes(j)]
 
         def up_grad(j):
-            term = dot_lt(nsl[j], hg[j])
-            gup[0] = term if j == 0 else gup[0] + term
+            for r in range(rows // 16):
+                last[16 * r : 16 * r + 16, :] = hg[j, rows:packed, r * rest : (r + 1) * rest]
+            term = dot_lt(nsl[j], hg[j, 0:rows, :])
+            end = dot_lt(nsl[j], last[...])
+            gup[0, :, 0:body] = term if j == 0 else gup[0, :, 0:body] + term
+            gup[0, :, body:hid] = end if j == 0 else gup[0, :, body:hid] + end
 
         def down_grad():
             total = dot_lt(act[0], ysl[0])
@@ -256,8 +300,11 @@
             slots(nsb, nrm[myrows, :])
             for t in range(1, n_right):
                 ring_step(chains, t)
-            pl.semaphore_signal(zgo, inc=1, device_id=(1, d, h), device_id_type=MESH)
+                if t == 2:
+                    pl.semaphore_signal(zgo, inc=1, device_id=(1, d, h), device_id_type=MESH)
             ring_last(chains)
+            for j in range(nd):
+                dtg[j] = wg[j, :, hid : 2 * hid]
             forward()
             down_sum()
             start(send_a, 0, nh)
@@ -265,23 +312,23 @@
             nsl[0, myrows, :] = nsb[d]
             pl.semaphore_wait(zgo, 1)
             ring_step(act_ring, 0)
-            arrived(cross_n, 1, nd)
+            arrived(cross_n)
             for j in range(1, nd):
                 nsl[j, myrows, :] = nzr[j]
-            sent(send_a, 0, nh)
+            sent(send_a)
             for t in range(1, n_right):
                 ring_step(act_ring, t)
             ring_last(act_ring)
             start(spread_n, 1, nh)
-            arrived(spread_n, 1, nh)
+            arrived(spread_n)
             ring_sent(chains)
             ring_sent(act_ring)
-            sent(cross_n, 1, nd)
-            sent(spread_n, 1, nh)
-            arrived(send_y, 0, nh)
+            sent(cross_n)
+            sent(spread_n)
+            arrived(send_y)
             backward()
             ring_step(hg_ring, 0)
-            arrived(cross_y1, 0, nd)
+            arrived(cross_y1)
             for j in range(nd):
                 ysl[j, myrows, :] = yzr[j]
             start(spread_y, 1, nh)
@@ -289,7 +336,7 @@
             for t in range(1, n_right):
                 ring_step(hg_ring, t)
                 if t == 2:
-                    arrived(spread_y, 1, nh)
+                    arrived(spread_y)
                     down_grad()
                 up_grad(t)
                 if t < n_left:
@@ -298,7 +345,7 @@
             for t in range(n_right, nd - n_left + 1):
                 up_grad(t)
             ring_sent(hg_ring)
-            sent(spread_y, 1, nh)
+            sent(spread_y)
 
         @pl.when(s == 1)
         def _():
@@ -330,10 +377,12 @@
             for t in range(n_right):
                 ring_step(chains, t)
             ring_last(chains)
+            for j in range(nd):
+                dtg[j] = wg[j, :, hid : 2 * hid]
             pl.semaphore_signal(zgo, inc=1, device_id=(0, d, h), device_id_type=MESH)
 
             total = xb[myrows, :].astype(F32)
-            arrived(send_a, 0, nh)
+            arrived(send_a)
             for k in range(nh):
                 total = total + rs_a[k].astype(F32)
             xrow[...] = total.astype(BF)
@@ -342,14 +391,14 @@
             start(send_n, 1, nh)
             slots(nsb, normed)
             start(cross_n, 1, nd)
-            both = dot(dng[0], neckv[0])
+            both = dot_lt(dtg[0], neckv[0])
             kept = dot(xrow[:, lanes(0)], neckv[0])
             for j in range(1, nd):
-                both = both + dot(dng[j], neckv[j])
+                both = both + dot_lt(dtg[j], neckv[j])
                 kept = kept + dot(xrow[:, lanes(j)], neckv[j])
             wv[...] = both.astype(BF)
             wl[...] = (both - wv[...].astype(F32)).astype(BF)
-            arrived(send_n, 1, nh)
+            arrived(send_n)
             forward()
             feat[...] = dot(act[0], wv[...]).astype(BF)
             feat[myrows, :] = (feat[myrows, :].astype(F32) + kept).astype(BF)
@@ -359,11 +408,11 @@
             wt[...] = wv[...].T
             wlt[...] = wl[...].T
             nsl[0, myrows, :] = nsb[d]
-            arrived(cross_n, 1, nd)
+            arrived(cross_n)
             for j in range(1, nd):
                 nsl[j, myrows, :] = nzr[j]
             total = ppart[myrois, :].astype(F32)
-            arrived(send_p, 1, nh)
+            arrived(send_p)
             for k in range(1, nh):
                 total = total + prec[k].astype(F32)
 
@@ -391,15 +440,15 @@
             ring_step(act_ring, 2)
             ring_step(act_ring, 3)
             ring_last(act_ring)
-            arrived(send_g, 1, nh)
+            arrived(send_g)
 
             feat[...] = dot(poolt[...], pg[...]).astype(BF)
             grad = dot(feat[...], wt[...]) + dot(feat[...], wlt[...])
-            hg[0] = (grad * slope[...]).astype(BF)
+            hidden = (grad * slope[...]).astype(BF)
+            keep_hidden(hidden)
             ring_step(hg_ring, 0)
-            hidden = hg[0]
-            for j in range(nd):
-                part[:, lanes(j)] = dot_rt(hidden, upg[j]).astype(BF)
+            for j in range(nd):
+                part[:, lanes(j)] = dot_rt(hidden, wg[j, :, 0:hid]).astype(BF)
             start(send_d, 1, nh)
             mine = feat[myrows, :]
             for j in range(nd):
@@ -410,7 +459,7 @@
             scaled, inv = norm_rows(xrow[...].astype(F32))
             total = part[myrows, :].astype(F32)
             ring_step(hg_ring, 1)
-            arrived(send_d, 1, nh)
+            arrived(send_d)
             for k in range(1, nh):
                 total = total + rs_d[k].astype(F32)
             mean_one = jnp.mean(total, axis=-1, keepdims=True)
@@ -422,30 +471,30 @@
             start(cross_y1, 0, nd)
             ring_step(hg_ring, 2)
             ysl[0, myrows, :] = ysb[d]
-            arrived(cross_y2, 1, nd)
+            arrived(cross_y2)
             for j in range(1, nd):
                 ysl[j, myrows, :] = yzr[j]
             start(spread_y, 1, nh)
-            arrived(spread_n, 1, nh)
+            arrived(spread_n)
             ring_step(hg_ring, 3)
             ring_last(hg_ring)
             for j in range(nd):
                 up_grad(j)
-            arrived(spread_y, 1, nh)
+            arrived(spread_y)
             down_grad()
-            sent(send_n, 1, nh)
-            sent(cross_n, 1, nd)
+            sent(send_n)
+            sent(cross_n)
             ring_sent(act_ring)
-            sent(send_p, 1, nh)
-            sent(spread_n, 1, nh)
-            sent(send_g, 1, nh)
+            sent(send_p)
+            sent(spread_n)
+            sent(send_g)
             ring_sent(chains)
             ring_sent(hg_ring)
-            sent(send_d, 1, nh)
-            sent(cross_y2, 1, nd)
-            sent(send_y, 0, nh)
-            sent(cross_y1, 0, nd)
-            sent(spread_y, 1, nh)
+            sent(send_d)
+            sent(cross_y2)
+            sent(send_y)
+            sent(cross_y1)
+            sent(spread_y)
 
     return kernel
 
@@ -461,9 +510,11 @@
         rb, qb = rows // nh, rois // nh
         vmem = pltpu.VMEM
         scratch = [
-            vmem((nd, wsl, hid), BF), vmem((nd, hid, wsl), BF), vmem((width, rows), BF),
+            vmem((nd, wsl, 2 * hid), BF), vmem((nd, wsl, hid), BF), vmem((wsl, hid), BF), vmem((hid, wsl), BF),
+            vmem((width, rows), BF),
             vmem((rows, width), BF), vmem((rows, width), BF),
-            vmem((rows, hid), F32), vmem((nd, rows, hid), BF), vmem((nd, rows, hid), BF), vmem((rows, width), BF),
+            vmem((rows, hid), F32), vmem((nd, rows, hid), BF), vmem((nd, rows + 16, hid // 128 * 128), BF),
+            vmem((rows, hid % 128), BF), vmem((rows, width), BF),
             vmem((nh, rb, width), BF), vmem((nh, rb, width), BF), vmem((rows, width), BF), vmem((rows, chan), BF),
             vmem((rois, chan), BF), vmem((nh, qb, chan), BF), vmem((rois, chan), BF),
             vmem((rb, width), BF), vmem((rb, width), BF),
@@ -475,8 +526,9 @@
             vmem((ksamp, rois), jnp.int32), vmem((1, rois), jnp.int32), vmem((levels, rois), jnp.int32),
             vmem((levels, rois, 128), F32), vmem((rois, rows), BF), vmem((rows, rois), BF),
             vmem((hid, chan), BF), vmem((hid, chan), BF), vmem((chan, hid), BF), vmem((chan, hid), BF),
-            pltpu.SemaphoreType.DMA((9,)), pltpu.SemaphoreType.DMA((15, 16)), pltpu.SemaphoreType.DMA((15, 16)),
-            pltpu.SemaphoreType.DMA((4, nd, 4)), pltpu.SemaphoreType.DMA((4, nd, 4)),
+            pltpu.SemaphoreType.DMA((9,)), pltpu.SemaphoreType.DMA((11,)), pltpu.SemaphoreType.DMA((11,)),
+            pltpu.SemaphoreType.DMA((3,)), pltpu.SemaphoreType.DMA((nd - 1, 3)), pltpu.SemaphoreType.DMA((nd - 1, 4)),
+            pltpu.SemaphoreType.DMA((nd - 1, 2)),
             pltpu.SemaphoreType.REGULAR,
         ]
         kernel = make_kernel(nd, nh, (rows, width, wsl, hid, chan, cls, levels, rois, ksamp))

time: 128 us -> 122 us (0.953)
  Pallas kernels: 126 us -> 120 us
    pallas_call x1, Pallas kernels: 124 us -> 118 us  [per_device(): pl.pallas_call(kernel, out_shape=(jax.ShapeDtypeStruct((1, wsl, hid), F32...]
where the time goes in v3:
time: 122 us; the launch traced here: 121 us
  Pallas kernels  120 us (98%)
    pallas_call x1, Pallas kernels, per_device(): pl.pallas_call(kernel, out_shape=(jax.ShapeDtypeStruct((1, wsl, hid), F32...  118 us

profile of v3, /device:TPU:32, one launch (start us, length us, event | category | flops | bytes accessed | tf_op | source)
XLA Modules:
  0.0 120.8 jit_solution(13968790752410151302)
XLA Ops:
  0.6 118.1 %window.1 = (f32[1,200,400]{2,1,0:T(8,128)}, f32[1,400,200]{2,1,0:T(8,128)}) custom-call(bf16[1600,256]{1,0:T(8,128)(2,1)} %bitcast.7, bf16[1,200,400]{2,1,0:T(8,128)(2,1)} %up.1, bf16[1,400,200]{2,1,0:T(8,128)(2,1)} %down.1, bf16[8,200,1024]{2,1,0:T(8,128)(2,1)} %bitcast.6, bf16[3,1024,1024]{2,1,0:T(8,128)(2,1)} %casc.1, bf16[3,80,1024]{2,1,0:T(8,128)(2,1)} %bitcast.8, ...), custom_call_target="tpu_custom_call" | custom-call | tf_op jit(solution)/shard_map/window/pallas_call | solution.py:535
  118.7 2.0 %hand_over.1 = (f32[1,200,400]{2,1,0:T(8,128)}, f32[1,400,200]{2,1,0:T(8,128)}) custom-call(f32[1,200,400]{2,1,0:T(8,128)} %get-tuple-element.4.up_in, f32[1,400,200]{2,1,0:T(8,128)} %get-tuple-element.5.down_in), custom_call_target="tpu_custom_call" | custom-call | tf_op jit(solution)/shard_map/hand_over/pallas_call | solution.py:552

commit v4 on v3

--- a/solution.py
+++ b/solution.py
@@ -62,11 +62,11 @@
 
     def kernel(
         tokens, up, down, neck, casc, clsw, bins, positive, targets, gup, gdn,
-        wg, dtg, upr, downr, xt, xb, nrm, slope, act, hg, last, part, rs_a, rs_d, yall, feat, ppart, prec, pg,
+        wg, dtg, upr, downr, xt, xb, nrm, slope, act, act_b, hg, last, part, rs_a, rs_d, yall, feat, ppart, prec, pg,
         xrow, yrow, nsb, nzr, nsl, ysb, ysb1, yzr, ysl, neckv, cascv, casct, clsr, clsv, clst, terms,
-        binv, posv, tarv, hits, poolv, poolt, wv, wl, wt, wlt, lsem, ss, rs, ring_ss, ring_w, ring_h, ring_a, zgo,
+        binv, posv, tarv, hits, poolv, poolt, wv, wl, wt, wlt, lsem, ss, rs, ring_ss, ring_w, ring_h, ring_a, ring_b, zgo,
     ):
-        ring_rs = (ring_w, ring_h, ring_a)
+        ring_rs = (ring_w, ring_h, ring_a, ring_b)
         s = lax.axis_index("section")
         d = lax.axis_index("dp")
         h = lax.axis_index("head")
@@ -232,6 +232,16 @@
         cross_y2 = column(9, lambda t: ysb.at[t], lambda k: yzr.at[k], 1, ysb.at[few], yzr.at[few])
         cross_y1 = column(10, lambda t: ysb1.at[t], lambda k: yzr.at[k], 0, ysb1, yzr)
         hg_ring = ring(1, hg, True, n_right, n_left, hg_cuts, hg.at[few])
+        act_b_ring = ring(3, act_b, True, n_right, n_left, act_cuts, act_b.at[few])
+        rounds = pl.ds(1, nd - 1)
+        lend = pltpu.make_async_remote_copy(
+            src_ref=act.at[0], dst_ref=act_b.at[0], send_sem=ss.at[11], recv_sem=rs.at[11],
+            device_id=(1 - s, d, h), device_id_type=MESH,
+        )
+        give_back = pltpu.make_async_remote_copy(
+            src_ref=act_b.at[rounds], dst_ref=act.at[rounds], send_sem=ss.at[12], recv_sem=rs.at[12],
+            device_id=(1 - s, d, h), device_id_type=MESH,
+        )
         act_ring = ring(2, act, True, n_left, n_right, act_cuts, act.at[few])
 
         def start(transfer, a, b):
@@ -298,8 +308,15 @@
             xb[...] = xt[...].T
             nrm[...] = norm_rows(xb[...].astype(F32))[0].astype(BF)
             slots(nsb, nrm[myrows, :])
+            nsl[0, myrows, :] = nsb[d]
+            start(cross_n, 1, nd)
             for t in range(1, n_right):
                 ring_step(chains, t)
+                if t == 1:
+                    arrived(cross_n)
+                    for j in range(1, nd):
+                        nsl[j, myrows, :] = nzr[j]
+                    start(spread_n, 1, nh)
                 if t == 2:
                     pl.semaphore_signal(zgo, inc=1, device_id=(1, d, h), device_id_type=MESH)
             ring_last(chains)
@@ -308,21 +325,20 @@
             forward()
             down_sum()
             start(send_a, 0, nh)
-            start(cross_n, 1, nd)
-            nsl[0, myrows, :] = nsb[d]
             pl.semaphore_wait(zgo, 1)
-            ring_step(act_ring, 0)
-            arrived(cross_n)
-            for j in range(1, nd):
-                nsl[j, myrows, :] = nzr[j]
-            sent(send_a)
-            for t in range(1, n_right):
+            for t in range(n_right):
                 ring_step(act_ring, t)
             ring_last(act_ring)
-            start(spread_n, 1, nh)
+            lend.wait_recv()
+            for t in range(n_right):
+                ring_step(act_b_ring, t)
+            ring_last(act_b_ring)
+            give_back.start()
             arrived(spread_n)
+            sent(send_a)
             ring_sent(chains)
             ring_sent(act_ring)
+            ring_sent(act_b_ring)
             sent(cross_n)
             sent(spread_n)
             arrived(send_y)
@@ -344,6 +360,7 @@
             ring_last(hg_ring)
             for t in range(n_right, nd - n_left + 1):
                 up_grad(t)
+            give_back.wait_send()
             ring_sent(hg_ring)
             sent(spread_y)
 
@@ -404,7 +421,7 @@
             feat[myrows, :] = (feat[myrows, :].astype(F32) + kept).astype(BF)
             ppart[...] = dot(poolv[...], feat[...]).astype(BF)
             start(send_p, 1, nh)
-            ring_step(act_ring, 0)
+            lend.start()
             wt[...] = wv[...].T
             wlt[...] = wl[...].T
             nsl[0, myrows, :] = nsb[d]
@@ -416,7 +433,6 @@
             for k in range(1, nh):
                 total = total + prec[k].astype(F32)
 
-            ring_step(act_ring, 1)
             start(spread_n, 1, nh)
 
             current = total.astype(BF)
@@ -437,9 +453,6 @@
                 running = running + terms[2 * j + 1]
             pg[myrois, :] = running.astype(BF)
             start(send_g, 1, nh)
-            ring_step(act_ring, 2)
-            ring_step(act_ring, 3)
-            ring_last(act_ring)
             arrived(send_g)
 
             feat[...] = dot(poolt[...], pg[...]).astype(BF)
@@ -480,11 +493,12 @@
             ring_last(hg_ring)
             for j in range(nd):
                 up_grad(j)
+            give_back.wait_recv()
             arrived(spread_y)
             down_grad()
             sent(send_n)
             sent(cross_n)
-            ring_sent(act_ring)
+            lend.wait_send()
             sent(send_p)
             sent(spread_n)
             sent(send_g)
@@ -513,7 +527,8 @@
             vmem((nd, wsl, 2 * hid), BF), vmem((nd, wsl, hid), BF), vmem((wsl, hid), BF), vmem((hid, wsl), BF),
             vmem((width, rows), BF),
             vmem((rows, width), BF), vmem((rows, width), BF),
-            vmem((rows, hid), F32), vmem((nd, rows, hid), BF), vmem((nd, rows + 16, hid // 128 * 128), BF),
+            vmem((rows, hid), F32), vmem((nd, rows, hid), BF), vmem((nd, rows, hid), BF),
+            vmem((nd, rows + 16, hid // 128 * 128), BF),
             vmem((rows, hid % 128), BF), vmem((rows, width), BF),
             vmem((nh, rb, width), BF), vmem((nh, rb, width), BF), vmem((rows, width), BF), vmem((rows, chan), BF),
             vmem((rois, chan), BF), vmem((nh, qb, chan), BF), vmem((rois, chan), BF),
@@ -526,9 +541,9 @@
             vmem((ksamp, rois), jnp.int32), vmem((1, rois), jnp.int32), vmem((levels, rois), jnp.int32),
             vmem((levels, rois, 128), F32), vmem((rois, rows), BF), vmem((rows, rois), BF),
             vmem((hid, chan), BF), vmem((hid, chan), BF), vmem((chan, hid), BF), vmem((chan, hid), BF),
-            pltpu.SemaphoreType.DMA((9,)), pltpu.SemaphoreType.DMA((11,)), pltpu.SemaphoreType.DMA((11,)),
-            pltpu.SemaphoreType.DMA((3,)), pltpu.SemaphoreType.DMA((nd - 1, 3)), pltpu.SemaphoreType.DMA((nd - 1, 4)),
-            pltpu.SemaphoreType.DMA((nd - 1, 2)),
+            pltpu.SemaphoreType.DMA((9,)), pltpu.SemaphoreType.DMA((13,)), pltpu.SemaphoreType.DMA((13,)),
+            pltpu.SemaphoreType.DMA((4,)), pltpu.SemaphoreType.DMA((nd - 1, 3)), pltpu.SemaphoreType.DMA((nd - 1, 4)),
+            pltpu.SemaphoreType.DMA((nd - 1, 2)), pltpu.SemaphoreType.DMA((nd - 1, 2)),
             pltpu.SemaphoreType.REGULAR,
         ]
         kernel = make_kernel(nd, nh, (rows, width, wsl, hid, chan, cls, levels, rois, ksamp))

time: 122 us -> 115 us (0.943); the launches traced: 121 us -> 115 us
  Pallas kernels: 120 us -> 114 us
    pallas_call x1, Pallas kernels: 118 us -> 112 us  [per_device(): pl.pallas_call(kernel, out_shape=(jax.ShapeDtypeStruct((1, wsl, hid), F32...]
where the time goes in v4:
time: 115 us
  Pallas kernels  114 us (99%)
    pallas_call x1, Pallas kernels, per_device(): pl.pallas_call(kernel, out_shape=(jax.ShapeDtypeStruct((1, wsl, hid), F32...  112 us

profile of v4, /device:TPU:32, one launch (start us, length us, event | category | flops | bytes accessed | tf_op | source)
XLA Modules:
  0.0 115.0 jit_solution(2546666817105718406)
XLA Ops:
  0.6 112.3 %window.1 = (f32[1,200,400]{2,1,0:T(8,128)}, f32[1,400,200]{2,1,0:T(8,128)}) custom-call(bf16[1600,256]{1,0:T(8,128)(2,1)} %bitcast.7, bf16[1,200,400]{2,1,0:T(8,128)(2,1)} %up.1, bf16[1,400,200]{2,1,0:T(8,128)(2,1)} %down.1, bf16[8,200,1024]{2,1,0:T(8,128)(2,1)} %bitcast.6, bf16[3,1024,1024]{2,1,0:T(8,128)(2,1)} %casc.1, bf16[3,80,1024]{2,1,0:T(8,128)(2,1)} %bitcast.8, ...), custom_call_target="tpu_custom_call" | custom-call | tf_op jit(solution)/shard_map/window/pallas_call | solution.py:550
  113.0 2.0 %hand_over.1 = (f32[1,200,400]{2,1,0:T(8,128)}, f32[1,400,200]{2,1,0:T(8,128)}) custom-call(f32[1,200,400]{2,1,0:T(8,128)} %get-tuple-element.4.up_in, f32[1,400,200]{2,1,0:T(8,128)} %get-tuple-element.5.down_in), custom_call_target="tpu_custom_call" | custom-call | tf_op jit(solution)/shard_map/hand_over/pallas_call | solution.py:567

commit v5 on v4

--- a/solution.py
+++ b/solution.py
@@ -259,6 +259,15 @@
         def lanes(j):
             return slice(j * wsl, (j + 1) * wsl)
 
+        def unpack(j):
+            place = lax.rem(d - j + nd, nd)
+            dtg[place] = wg[place, :, hid : 2 * hid]
+
+        def unpack_step(t):
+            unpack(t)
+            if 0 < t < n_left:
+                unpack(nd - t)
+
         def forward():
             before = dot(nrm[:, lanes(0)], wg[0, :, 0:hid])
             for j in range(1, nd):
@@ -304,6 +313,7 @@
         @pl.when(s == 0)
         def _():
             ring_step(chains, 0)
+            unpack_step(0)
             load_tok.wait()
             xb[...] = xt[...].T
             nrm[...] = norm_rows(xb[...].astype(F32))[0].astype(BF)
@@ -312,6 +322,7 @@
             start(cross_n, 1, nd)
             for t in range(1, n_right):
                 ring_step(chains, t)
+                unpack_step(t)
                 if t == 1:
                     arrived(cross_n)
                     for j in range(1, nd):
@@ -320,8 +331,8 @@
                 if t == 2:
                     pl.semaphore_signal(zgo, inc=1, device_id=(1, d, h), device_id_type=MESH)
             ring_last(chains)
-            for j in range(nd):
-                dtg[j] = wg[j, :, hid : 2 * hid]
+            for t in range(n_right, nd - n_left + 1):
+                unpack(t)
             forward()
             down_sum()
             start(send_a, 0, nh)
@@ -351,12 +362,11 @@
             up_grad(0)
             for t in range(1, n_right):
                 ring_step(hg_ring, t)
-                if t == 2:
-                    arrived(spread_y)
-                    down_grad()
                 up_grad(t)
                 if t < n_left:
                     up_grad(nd - t)
+            arrived(spread_y)
+            down_grad()
             ring_last(hg_ring)
             for t in range(n_right, nd - n_left + 1):
                 up_grad(t)
@@ -393,9 +403,10 @@
             pl.semaphore_wait(zgo, 1)
             for t in range(n_right):
                 ring_step(chains, t)
+                unpack_step(t)
             ring_last(chains)
-            for j in range(nd):
-                dtg[j] = wg[j, :, hid : 2 * hid]
+            for t in range(n_right, nd - n_left + 1):
+                unpack(t)
             pl.semaphore_signal(zgo, inc=1, device_id=(0, d, h), device_id_type=MESH)
 
             total = xb[myrows, :].astype(F32)
@@ -458,11 +469,11 @@
             feat[...] = dot(poolt[...], pg[...]).astype(BF)
             grad = dot(feat[...], wt[...]) + dot(feat[...], wlt[...])
             hidden = (grad * slope[...]).astype(BF)
-            keep_hidden(hidden)
-            ring_step(hg_ring, 0)
             for j in range(nd):
                 part[:, lanes(j)] = dot_rt(hidden, wg[j, :, 0:hid]).astype(BF)
             start(send_d, 1, nh)
+            keep_hidden(hidden)
+            ring_step(hg_ring, 0)
             mine = feat[myrows, :]
             for j in range(nd):
                 piece = dot_rt(mine, neckv[j]).astype(BF)

time: 115 us -> 114 us (level)
    pallas_call x1, Pallas kernels: 112 us -> 111 us  [per_device(): pl.pallas_call(kernel, out_shape=(jax.ShapeDtypeStruct((1, wsl, hid), F32...]
where the time goes in v5:
time: 114 us; the launch traced here: 113 us
  Pallas kernels  113 us (99%)
    pallas_call x1, Pallas kernels, per_device(): pl.pallas_call(kernel, out_shape=(jax.ShapeDtypeStruct((1, wsl, hid), F32...  111 us

profile of v5, /device:TPU:32, one launch (start us, length us, event | category | flops | bytes accessed | tf_op | source)
XLA Modules:
  0.0 113.2 jit_solution(13779856314129057231)
XLA Ops:
  0.6 110.5 %window.1 = (f32[1,200,400]{2,1,0:T(8,128)}, f32[1,400,200]{2,1,0:T(8,128)}) custom-call(bf16[1600,256]{1,0:T(8,128)(2,1)} %bitcast.7, bf16[1,200,400]{2,1,0:T(8,128)(2,1)} %up.1, bf16[1,400,200]{2,1,0:T(8,128)(2,1)} %down.1, bf16[8,200,1024]{2,1,0:T(8,128)(2,1)} %bitcast.6, bf16[3,1024,1024]{2,1,0:T(8,128)(2,1)} %casc.1, bf16[3,80,1024]{2,1,0:T(8,128)(2,1)} %bitcast.8, ...), custom_call_target="tpu_custom_call" | custom-call | tf_op jit(solution)/shard_map/window/pallas_call | solution.py:561
  111.2 2.0 %hand_over.1 = (f32[1,200,400]{2,1,0:T(8,128)}, f32[1,400,200]{2,1,0:T(8,128)}) custom-call(f32[1,200,400]{2,1,0:T(8,128)} %get-tuple-element.4.up_in, f32[1,400,200]{2,1,0:T(8,128)} %get-tuple-element.5.down_in), custom_call_target="tpu_custom_call" | custom-call | tf_op jit(solution)/shard_map/hand_over/pallas_call | solution.py:578

commit v6 on v5

--- a/solution.py
+++ b/solution.py
@@ -171,9 +171,13 @@
             pl.semaphore_signal(barrier, inc=1, device_id=(s, lax.rem(d + k, nd), h), device_id_type=MESH)
             pl.semaphore_signal(barrier, inc=1, device_id=(1 - s, lax.rem(d + k, nd), h), device_id_type=MESH)
 
-        loop(1, nd, greet_column)
-        loop(1, nh, greet_plane)
-        loop(0, nh, greet_plane_other)
+        for k in far_plane:
+            greet_plane_other(k)
+            if k > 0:
+                greet_plane(k)
+        for k in far_column:
+            if k > 0:
+                greet_column(k)
 
         load_tok = pltpu.make_async_copy(tokens, xt, lsem.at[2])
         load_neck = pltpu.make_async_copy(neck, neckv, lsem.at[3])
@@ -198,7 +202,7 @@
         all_of = slice(None)
         mid = 4 * 128
         w_cuts = [(all_of, slice(0, 256)), (all_of, slice(256, mid)), (all_of, slice(mid, 2 * hid))]
-        hg_cuts = [(pl.ds(a, n),) for a, n in row_cuts(packed, 4)]
+        hg_cuts = [(pl.ds(a, n),) for a, n in row_cuts(packed, 6)]
         act_cuts = [(pl.ds(a, n),) for a, n in row_cuts(rows, 2)]
         chains = ring(0, wg, False, n_right, n_left, w_cuts, wg.at[pl.ds(0, nd - 1)])
 
@@ -553,7 +557,7 @@
             vmem((levels, rois, 128), F32), vmem((rois, rows), BF), vmem((rows, rois), BF),
             vmem((hid, chan), BF), vmem((hid, chan), BF), vmem((chan, hid), BF), vmem((chan, hid), BF),
             pltpu.SemaphoreType.DMA((9,)), pltpu.SemaphoreType.DMA((13,)), pltpu.SemaphoreType.DMA((13,)),
-            pltpu.SemaphoreType.DMA((4,)), pltpu.SemaphoreType.DMA((nd - 1, 3)), pltpu.SemaphoreType.DMA((nd - 1, 4)),
+            pltpu.SemaphoreType.DMA((4,)), pltpu.SemaphoreType.DMA((nd - 1, 3)), pltpu.SemaphoreType.DMA((nd - 1, 6)),
             pltpu.SemaphoreType.DMA((nd - 1, 2)), pltpu.SemaphoreType.DMA((nd - 1, 2)),
             pltpu.SemaphoreType.REGULAR,
         ]

time: 114 us -> 113 us (level)
  no operation moved by 1% of the time
where the time goes in v6:
time: 113 us
  Pallas kernels  112 us (99%)
    pallas_call x1, Pallas kernels, per_device(): pl.pallas_call(kernel, out_shape=(jax.ShapeDtypeStruct((1, wsl, hid), F32...  110 us

profile of v6, /device:TPU:32, one launch (start us, length us, event | category | flops | bytes accessed | tf_op | source)
XLA Modules:
  0.0 112.7 jit_solution(1042923566095921387)
XLA Ops:
  0.6 110.0 %window.1 = (f32[1,200,400]{2,1,0:T(8,128)}, f32[1,400,200]{2,1,0:T(8,128)}) custom-call(bf16[1600,256]{1,0:T(8,128)(2,1)} %bitcast.7, bf16[1,200,400]{2,1,0:T(8,128)(2,1)} %up.1, bf16[1,400,200]{2,1,0:T(8,128)(2,1)} %down.1, bf16[8,200,1024]{2,1,0:T(8,128)(2,1)} %bitcast.6, bf16[3,1024,1024]{2,1,0:T(8,128)(2,1)} %casc.1, bf16[3,80,1024]{2,1,0:T(8,128)(2,1)} %bitcast.8, ...), custom_call_target="tpu_custom_call" | custom-call | tf_op jit(solution)/shard_map/window/pallas_call | solution.py:565
  110.6 2.0 %hand_over.1 = (f32[1,200,400]{2,1,0:T(8,128)}, f32[1,400,200]{2,1,0:T(8,128)}) custom-call(f32[1,200,400]{2,1,0:T(8,128)} %get-tuple-element.4.up_in, f32[1,400,200]{2,1,0:T(8,128)} %get-tuple-element.5.down_in), custom_call_target="tpu_custom_call" | custom-call | tf_op jit(solution)/shard_map/hand_over/pallas_call | solution.py:582
